TPU v7x, 128 devices: a whole 4x4x4 slice. The times are simulated.
128 devices in a mesh: item: 32 (over z, x, core), req: 4 (over y).
Axes of the slice: x: 4, y: 4, z: 4, core: 2. Of those that a mesh axis runs over, the one named last changes fastest.
Arguments:
- user_emb: bfloat16 [128, 256], P('req'), may hold values from -6 to 6
- codebooks: bfloat16 [32, 256, 8], P('item'), may hold values from -1 to 1
- item_codes: int32 [131072, 32], P('item'), may hold values from 0 to 255
- item_place: int32 [131072], replicated, may hold values from 0 to 131071, as said below
- candidates: int32 [128, 512], P('req', 'item'), may hold values from 0 to 131071, as said below
- item_features: bfloat16 [131072, 768], P(('item', 'req')), may hold values from -6 to 6
- cross_weights: bfloat16 [4, 1024, 1024], replicated, may hold values from -0.25 to 0.25
- cross_bias: float32 [4, 1024], replicated, may hold values from -6 to 6
- out_weight: float32 [1024], replicated, may hold values from -0.5 to 0.5
Outputs:
- scores: float32 [128, 131072], P('req', 'item')
- logits: float32 [128, 512], P('req', 'item')
Inputs may be any that keep to these rules, and one draw needn't show every extreme that they name: A permutation of the item ids: item_place[i] is the storage row of item i; storage row s is held by the device at flat index s // 1024 of item+req (item slowest). Item ids. In each aligned block of 32 requests by 16 candidates (one device's share), at most 12 candidates have storage rows on any one owner; in every draw one owner, the same for all blocks, is named exactly 12 times in every block.
All inputs are finite; a program needn't handle non-finite values.
Results may differ from a plain program's by a relative error of at most 0.0033.
Values may be sent and summed in bfloat16 or wider, within the bound.
No kernel may reach another device: no remote copies, remote signals or barrier semaphores. Data moves between devices by JAX's collectives and lax.ppermute only.
A program may use at most 64 MiB of HBM per device.

v0:
```python
import jax
import jax.numpy as jnp
from jax import lax
from jax.sharding import PartitionSpec as P

M = 32


def score_tables(total, tables, item_codes):
    width_all = tables.shape[1]
    codes_count = tables.shape[2]
    code_range = lax.iota(jnp.int32, codes_count)[None, None, :]
    for group in range(0, width_all, 4):
        width = min(4, width_all - group)
        codes_now = lax.dynamic_slice_in_dim(item_codes, group, width, 1)
        onehot = (codes_now[:, :, None] == code_range).astype(jnp.bfloat16)
        total = total + jnp.einsum(
            "rmk,imk->ri",
            tables[:, group : group + width],
            onehot,
            preferred_element_type=jnp.float32,
        )
    return total


def on_device(
    user_emb,
    codebooks,
    item_codes,
    item_place,
    candidates,
    item_features,
    cross_weights,
    cross_bias,
    out_weight,
):
    requests = user_emb.shape[0]
    local_sub = codebooks.shape[0]
    sub_width = codebooks.shape[2]
    parts = user_emb.reshape(requests, M, sub_width)
    empty = jnp.zeros((requests, item_codes.shape[0]), jnp.float32)
    first_sub = lax.axis_index("item") * local_sub
    mine = lax.dynamic_slice_in_dim(parts, first_sub, local_sub, 1)
    tables = jnp.einsum("rms,mks->rmk", mine, codebooks, preferred_element_type=jnp.float32).astype(
        jnp.bfloat16
    )
    scores = score_tables(empty, lax.all_gather(tables, "item", axis=1, tiled=True), item_codes)
    cand_dev = candidates.shape[1]
    rows_dev = item_features.shape[0]
    item_count = lax.axis_size("item")
    req_count = lax.axis_size("req")
    owners = item_count * req_count
    total_rows = requests * cand_dev
    capacity = 3 * total_rows // owners
    slots = jnp.take(item_place, candidates.reshape(-1), axis=0)
    owner = slots // rows_dev
    within = slots % rows_dev
    owner_hits = (owner[:, None] == jnp.arange(owners, dtype=jnp.int32)[None, :]).astype(jnp.int32)
    ranks = jnp.sum((jnp.cumsum(owner_hits, axis=0) - owner_hits) * owner_hits, axis=1)
    wanted = jnp.zeros((owners, capacity), jnp.int32).at[owner, ranks].set(within)
    found = jnp.take(
        item_features,
        lax.all_to_all(wanted, ("item", "req"), split_axis=0, concat_axis=0, tiled=True),
        axis=0,
    )
    fetched = lax.all_to_all(found, ("item", "req"), split_axis=0, concat_axis=0, tiled=True)
    item_rows = fetched[owner, ranks]
    repeated = jnp.repeat(user_emb, cand_dev, axis=0)
    first = jnp.concatenate([repeated, item_rows], axis=1)
    state = first.astype(jnp.float32)
    for layer in range(cross_weights.shape[0]):
        product = (
            jnp.dot(
                state.astype(jnp.bfloat16), cross_weights[layer], preferred_element_type=jnp.float32
            )
            + cross_bias[layer]
        )
        state = first * product + state
    logits = jnp.sum(state * out_weight, axis=1).reshape(requests, cand_dev)
    return (scores, logits)


def solution(mesh):
    placed = (
        P("req", None),
        P("item", None, None),
        P("item", None),
        P(),
        P("req", "item"),
        P(("item", "req"), None),
        P(),
        P(),
        P(),
    )
    return jax.shard_map(
        on_device,
        mesh=mesh,
        in_specs=placed,
        out_specs=(P("req", "item"), P("req", "item")),
        check_vma=False,
    )
```

profile of v0, /device:TPU:1, one launch (start us, length us, event | category | flops | bytes accessed | tf_op | source)
XLA Modules:
  0.0 162.4 jit_solution(7211599996360040882)
XLA Ops:
  0.6 0.9 copy.22
  1.8 6.5 %gather_fusion = s32[512]{0:T(512)S(1)} fusion(s32[131072]{0:T(1024)} %param.12, s32[1024]{0:T(1024)S(1)} %pad_clamp_fusion.1), kind=kCustom, calls=%fused_computation | custom fusion | bytes 6144 | tf_op jit(solution)/shard_map/jit(_take)/gather | solution.py:55
  9.1 24.6 %scatter_fusion = s32[128,12]{0,1:T(8,128)S(1)} fusion(s32[128,12]{0,1:T(8,128)S(1)} %broadcast_in_dim.27, s32[512]{0:T(512)S(1)} %bitcast.106, s32[512]{0:T(512)S(1)} %get-tuple-element.20), kind=kCustom, calls=%fused_computation.3 | custom fusion | bytes 10240 | tf_op jit(solution)/shard_map/scatter | solution.py:60
  33.7 0.7 copy.27
  34.5 11.5 %all-to-all-start = ((s32[128,1,12]{2,1,0:T(1,128)}), s32[128,1,12]{2,1,0:T(1,128)S(1)}, u32[]{:S(2)}, u32[]{:S(2)}) async-start(s32[128,1,12]{2,1,0:T(1,128)} %copy.27), calls=%async_computation | async-start | bytes 131072 | tf_op jit(solution)/shard_map/all_to_all | solution.py:63
  46.4 25.8 %all_gather.3 = bf16[32,32,256]{2,0,1:T(8,128)(2,1)S(1)} all-gather(bf16[32,1,256]{2,0,1:T(8,128)(2,1)S(1)} %fusion.55), channel_id=1, replica_groups=mesh['item'=32,'req'=4] {'item'}, dimensions={1}, use_global_device_ids=true | all-gather | bytes 540672 | tf_op jit(solution)/shard_map/all_gather | solution.py:47
  72.3 5.7 %gather_fusion.1 = bf16[1536,768]{1,0:T(8,128)(2,1)} fusion(bf16[1024,768]{1,0:T(8,128)(2,1)S(1)} %copy-done, s32[2048]{0:T(1024)S(1)} %pad_clamp_fusion), kind=kCustom, calls=%fused_computation.1 | custom fusion | bytes 4724736 | tf_op jit(solution)/shard_map/jit(_take)/gather | solution.py:61
  78.0 4.9 %reshape.247 = bf16[128,12,768]{2,1,0:T(8,128)(2,1)} reshape(bf16[1536,768]{1,0:T(8,128)(2,1)} %gather_fusion.1) | data formatting | bytes 4718592 | tf_op jit(solution)/shard_map/jit(_take)/gather | solution.py:61
  83.1 3.3 %broadcast_select_fusion = bf16[128,12,768]{2,1,0:T(8,128)(2,1)} fusion(bf16[128,12,768]{2,1,0:T(8,128)(2,1)} %reshape.247, pred[128,12]{1,0:T(8,128)(4,1)S(1)} %copy.29), kind=kLoop, calls=%fused_computation.48 | loop fusion | flops 1179648 | bytes 4720128 | tf_op jit(solution)/shard_map/jit(_take)/select_n | solution.py:61
  86.4 7.5 %all-to-all-start.1 = ((bf16[128,12,768]{2,1,0:T(8,128)(2,1)}), bf16[128,12,768]{2,1,0:T(8,128)(2,1)}, u32[]{:S(2)}, u32[]{:S(2)}) async-start(bf16[128,12,768]{2,1,0:T(8,128)(2,1)} %broadcast_select_fusion), calls=%async_computation.1 | async-start | bytes 6291456 | tf_op jit(solution)/shard_map/all_to_all | solution.py:66
  94.0 5.9 %fusion.16 = f32[32,4096]{1,0:T(8,128)S(1)} fusion(bf16[32,32,256]{2,0,1:T(8,128)(2,1)S(1)} %all_gather.3, s32[4096,4]{0,1:T(4,128)S(1)} %get-tuple-element.14), kind=kOutput, calls=%fused_computation.28 | convolution fusion | flops 272629760 | bytes 1114112 | tf_op jit(solution)/shard_map/rmk,imk->ri/dot_general | solution.py:17
  99.9 5.9 %fusion.17 = f32[32,4096]{1,0:T(8,128)S(1)} fusion(bf16[32,32,256]{2,0,1:T(8,128)(2,1)S(1)} %all_gather.3, s32[4096,4]{0,1:T(4,128)S(1)} %get-tuple-element.15), kind=kOutput, calls=%fused_computation.29 | convolution fusion | flops 272629760 | bytes 1114112 | tf_op jit(solution)/shard_map/rmk,imk->ri/dot_general | solution.py:17
  105.8 5.9 %fusion.18 = f32[32,4096]{1,0:T(8,128)S(1)} fusion(bf16[32,32,256]{2,0,1:T(8,128)(2,1)S(1)} %all_gather.3, s32[4096,4]{0,1:T(4,128)S(1)} %get-tuple-element.9), kind=kOutput, calls=%fused_computation.30 | convolution fusion | flops 272629760 | bytes 1114112 | tf_op jit(solution)/shard_map/rmk,imk->ri/dot_general | solution.py:17
  111.8 5.9 %fusion.19 = f32[32,4096]{1,0:T(8,128)S(1)} fusion(bf16[32,32,256]{2,0,1:T(8,128)(2,1)S(1)} %all_gather.3, s32[4096,4]{0,1:T(4,128)S(1)} %get-tuple-element.10), kind=kOutput, calls=%fused_computation.31 | convolution fusion | flops 272629760 | bytes 1114112 | tf_op jit(solution)/shard_map/rmk,imk->ri/dot_general | solution.py:17
  117.7 5.9 %fusion.20 = f32[32,4096]{1,0:T(8,128)S(1)} fusion(bf16[32,32,256]{2,0,1:T(8,128)(2,1)S(1)} %all_gather.3, s32[4096,4]{0,1:T(4,128)S(1)} %get-tuple-element.11), kind=kOutput, calls=%fused_computation.32 | convolution fusion | flops 272629760 | bytes 1114112 | tf_op jit(solution)/shard_map/rmk,imk->ri/dot_general | solution.py:17
  123.7 5.9 %fusion.21 = f32[32,4096]{1,0:T(8,128)S(1)} fusion(bf16[32,32,256]{2,0,1:T(8,128)(2,1)S(1)} %all_gather.3, s32[4096,4]{0,1:T(4,128)S(1)} %get-tuple-element.12), kind=kOutput, calls=%fused_computation.33 | convolution fusion | flops 272629760 | bytes 1114112 | tf_op jit(solution)/shard_map/rmk,imk->ri/dot_general | solution.py:17
  129.6 5.9 %fusion.22 = f32[32,4096]{1,0:T(8,128)S(1)} fusion(bf16[32,32,256]{2,0,1:T(8,128)(2,1)S(1)} %all_gather.3, s32[4096,4]{0,1:T(4,128)S(1)} %get-tuple-element.13), kind=kOutput, calls=%fused_computation.34 | convolution fusion | flops 272629760 | bytes 1114112 | tf_op jit(solution)/shard_map/rmk,imk->ri/dot_general | solution.py:17
  135.6 5.5 %fusion.30 = f32[32,4096]{1,0:T(8,128)} fusion(f32[32,4096]{1,0:T(8,128)S(1)} %fusion.16, f32[32,4096]{1,0:T(8,128)S(1)} %fusion.17, f32[32,4096]{1,0:T(8,128)S(1)} %fusion.18, f32[32,4096]{1,0:T(8,128)S(1)} %fusion.19, f32[32,4096]{1,0:T(8,128)S(1)} %fusion.20, f32[32,4096]{1,0:T(8,128)S(1)} %fusion.21, f32[32,4096]{1,0:T(8,128)S(1)} %fusion.22, ...), kind=kOutput, calls=%fused_computation.42 | convolution fusion | flops 273547264 | bytes 4784128 | tf_op jit(solution)/shard_map/rmk,imk->ri/dot_general | solution.py:17
  141.0 4.1 %copy.30 = bf16[128,12,768]{2,0,1:T(8,128)(2,1)} copy(bf16[128,12,768]{2,1,0:T(8,128)(2,1)} %all-to-all-done.1) | data formatting | bytes 4718592 | tf_op jit(solution)/shard_map/all_to_all | solution.py:66
  145.1 7.3 %gather_fusion.2 = bf16[512,768]{1,0:T(8,128)(2,1)S(1)} fusion(bf16[128,12,768]{2,0,1:T(8,128)(2,1)} %copy.30, s32[512]{0:T(512)S(1)} %bitcast.105), kind=kCustom, calls=%fused_computation.2 | custom fusion | bytes 1576960 | tf_op jit(solution)/shard_map/gather | solution.py:67
  152.4 3.0 %fusion.42 = f32[512,1024]{1,0:T(8,128)S(1)} fusion(bf16[4,1024,1024]{2,1,0:T(8,128)(2,1)} %param.15, bf16[512,768]{1,0:T(8,128)(2,1)S(1)} %gather_fusion.2, bf16[512,256]{1,0:T(8,128)(2,1)S(1)} %bitcast.110), kind=kOutput, calls=%fused_computation.60 | convolution fusion | flops 1075838976 | bytes 5242880 | tf_op jit(solution)/shard_map/dot_general | solution.py:73
  155.5 3.2 %fusion.31 = f32[512,1024]{1,0:T(8,128)S(1)} fusion(f32[512,1024]{1,0:T(8,128)S(1)} %fusion.42, bf16[4,1024,1024]{2,1,0:T(8,128)(2,1)} %param.15, f32[1024]{0:T(1024)S(1)} %bitcast.121, f32[1024]{0:T(1024)S(1)} %bitcast.122, bf16[512,768]{1,0:T(8,128)(2,1)S(1)} %gather_fusion.2, bf16[512,256]{1,0:T(8,128)(2,1)S(1)} %bitcast.111), kind=kOutput, calls=%fused_computation.49 | convolution fusion | flops 1083179008 | bytes 10498048 | tf_op jit(solution)/shard_map/dot_general | solution.py:73
  158.8 1.3 fusion.32
  160.1 1.5 fusion.35
  (50 shorter events, 2.5 us)
Async XLA Ops:
  0.6 71.7 %copy-start = (bf16[1024,768]{1,0:T(8,128)(2,1)S(1)}, bf16[1024,768]{1,0:T(8,128)(2,1)}, u32[]{:S(2)}) copy-start(bf16[1024,768]{1,0:T(8,128)(2,1)} %param.14) | copy-start | bytes 4718596
  9.1 36.9 %copy-start.2 = (bf16[32,256]{1,0:T(8,128)(2,1)S(1)}, bf16[32,256]{1,0:T(8,128)(2,1)}, u32[]{:S(2)}) copy-start(bf16[32,256]{1,0:T(8,128)(2,1)} %param.9) | copy-start | bytes 49156
  9.1 37.0 %copy-start.1 = (s32[4096,32]{0,1:T(8,128)S(1)}, s32[4096,32]{0,1:T(8,128)}, u32[]{:S(2)}) copy-start(s32[4096,32]{0,1:T(8,128)} %param.11) | copy-start | bytes 1572868
  9.1 37.1 %copy-start.4 = (bf16[1,256,8]{1,2,0:T(8,128)(2,1)S(1)}, bf16[1,256,8]{1,2,0:T(8,128)(2,1)}, u32[]{:S(2)}) copy-start(bf16[1,256,8]{1,2,0:T(8,128)(2,1)} %param.10) | copy-start | bytes 12292
  34.5 37.7 %all-to-all-start = ((s32[128,1,12]{2,1,0:T(1,128)}), s32[128,1,12]{2,1,0:T(1,128)S(1)}, u32[]{:S(2)}, u32[]{:S(2)}) async-start(s32[128,1,12]{2,1,0:T(1,128)} %copy.27), calls=%async_computation | async-start | bytes 131072 | tf_op jit(solution)/shard_map/all_to_all | solution.py:63
  86.4 7.5 %copy-start.3 = (f32[4,1024]{1,0:T(4,128)S(1)}, f32[4,1024]{1,0:T(4,128)}, u32[]{:S(2)}) copy-start(f32[4,1024]{1,0:T(4,128)} %param.16) | copy-start | bytes 49156
  86.4 54.6 %all-to-all-start.1 = ((bf16[128,12,768]{2,1,0:T(8,128)(2,1)}), bf16[128,12,768]{2,1,0:T(8,128)(2,1)}, u32[]{:S(2)}, u32[]{:S(2)}) async-start(bf16[128,12,768]{2,1,0:T(8,128)(2,1)} %broadcast_select_fusion), calls=%async_computation.1 | async-start | bytes 6291456 | tf_op jit(solution)/shard_map/all_to_all | solution.py:66
  152.4 6.3 %slice-start = ((s8[8388608]{0:T(1024)(128)(4,1)}), s8[4194304]{0:T(1024)(128)(4,1)S(1)}, s32[]{:S(2)}) async-start(s8[8388608]{0:T(1024)(128)(4,1)} %bitcast.123), calls=%async_computation.2 | async-start | bytes 8388608
  155.5 3.3 %slice-start.1 = ((s8[8388608]{0:T(1024)(128)(4,1)}), s8[4194304]{0:T(1024)(128)(4,1)S(1)}, s32[]{:S(2)}) async-start(s8[8388608]{0:T(1024)(128)(4,1)} %bitcast.123), calls=%async_computation.3 | async-start | bytes 8388608
  158.7 1.4 copy-start.5
where the time goes:
time: 163 us; the launch traced here: 162 us
  local copies, waits for them, and re-layouts  56.4 us (35%)
  matrix products  56.4 us (35%)
  blocking collectives  25.8 us (16%)
  starting transfers between devices  19 us (12%)
  other arithmetic  3.91 us (2%)
    dot_general x8, matrix products, score_tables(): jnp.einsum('rmk,imk->ri', tables[:, group:group + width], onehot, preferr...  47 us
    all_gather x1, blocking collectives, on_device(): lax.all_gather(tables, 'item', axis=1, tiled=True)  25.8 us
    scatter x1, local copies, waits for them, and re-layouts, on_device(): jnp.zeros((owners, capacity), jnp.int32).at[owner, ranks].set(within)  24.6 us
    all_to_all x1, starting transfers between devices, on_device(): lax.all_to_all(wanted, ('item', 'req'), split_axis=0, concat_axis=0, tile...  11.5 us
    gather x2, local copies, waits for them, and re-layouts, on_device(): jnp.take(item_features, lax.all_to_all(wanted, ('item', 'req'), split_axi...  10.5 us
    dot_general x4, matrix products, on_device(): jnp.dot(state.astype(jnp.bfloat16), cross_weights[layer], preferred_eleme...  9.13 us
    all_to_all x1, starting transfers between devices, on_device(): lax.all_to_all(found, ('item', 'req'), split_axis=0, concat_axis=0, tiled...  7.49 us
    gather x1, local copies, waits for them, and re-layouts, on_device(): item_rows = fetched[owner, ranks]  7.29 us
  transfers between devices with their start and end apart: 2, of which 0 were waited for; matrix products, arithmetic and copies ran while one was open for 29% of the time, Pallas kernels for 0%

commit v1 on v0

v1 whole, which is shorter than its diff:
```python
import functools

import jax
import jax.numpy as jnp
from jax import lax
from jax.experimental import pallas as pl
from jax.experimental.pallas import tpu as pltpu
from jax.sharding import PartitionSpec as P

F32 = jnp.float32
BF16 = jnp.bfloat16
I32 = jnp.int32
VMEM = pl.BlockSpec(memory_space=pltpu.VMEM)
LANES = 128
MSG = 8
CB_ROWS = 4
USER_ROW = 4
WANT_ROW = 6
HALF = 64


def dot(a, b, dims=(((1,), (0,)), ((), ()))):
    return lax.dot_general(a, b, dims, preferred_element_type=F32)


def iota(shape, axis):
    return lax.broadcasted_iota(I32, shape, axis)


def lane_sum(x):
    return jnp.sum(x, axis=1, keepdims=True)


def as_bf16(mask):
    return jnp.where(mask, 1.0, 0.0).astype(BF16)


def prepare_kernel(cand, place, codebook, user, message, meta, tiles):
    cand_dev, requests = cand.shape
    total = cand_dev * requests
    owners = message.shape[0]
    blocks = place.shape[0]
    item = lax.axis_index("item")
    req = lax.axis_index("req")
    ids = cand[...].astype(F32)
    spread = jnp.concatenate(
        [jnp.broadcast_to(ids[c : c + 1, :], (requests, requests)) for c in range(cand_dev)], axis=0
    )
    own_request = iota((total, requests), 0) % requests
    diagonal = own_request == iota((total, requests), 1)
    ids = lane_sum(jnp.where(diagonal, spread, 0.0)).astype(I32)
    where_row = as_bf16((ids >> 7) == iota((total, blocks), 1))
    stored = place[...]
    parts = jnp.concatenate(
        [
            (stored & 255).astype(F32).astype(BF16),
            ((stored >> 8) & 255).astype(F32).astype(BF16),
            (stored >> 16).astype(F32).astype(BF16),
        ],
        axis=1,
    )
    found = dot(where_row, parts)
    found = found[:, :LANES] + 256.0 * found[:, LANES : 2 * LANES] + 65536.0 * found[:, 2 * LANES :]
    lane = iota((total, LANES), 1)
    slot = lane_sum(jnp.where((ids & 127) == lane, found, 0.0)).astype(I32)
    rows_dev = blocks * LANES // owners
    shift = rows_dev.bit_length() - 1
    owner = slot >> shift
    within = slot & (rows_dev - 1)
    hit = owner == lane
    hits = as_bf16(hit)
    earlier = as_bf16(iota((total, total), 1) < iota((total, total), 0))
    rank = lane_sum(jnp.where(hit, dot(earlier, hits), 0.0)).astype(I32)
    meta[...] = jnp.where(lane == 0, owner, rank)
    request = iota((total, 1), 0) % requests
    low = (within & 255).astype(F32)
    high = ((within >> 8) + 4 * request + 128).astype(F32)
    entry = jnp.where(lane == rank, low, 0.0) + jnp.where(lane == rank + HALF, high, 0.0)
    wanted = dot(hits, entry.astype(BF16), (((0,), (0,)), ((), ())))
    book = codebook[...].astype(F32)
    sub = iota(book.shape, 0)
    first = jnp.sum(jnp.where(sub == 2 * req, book, 0.0), axis=0, keepdims=True)
    second = jnp.sum(jnp.where(sub == 2 * req + 1, book, 0.0), axis=0, keepdims=True)
    people = user[...].astype(F32)
    person = jnp.sum(jnp.where(iota(people.shape, 0) == item, people, 0.0), axis=0, keepdims=True)
    tile = jnp.concatenate(
        [
            first[:, :LANES],
            first[:, LANES:],
            second[:, :LANES],
            second[:, LANES:],
            person[:, :LANES],
            person[:, LANES:],
            jnp.zeros((2, LANES), F32),
        ],
        axis=0,
    )
    tiles[...] = jnp.broadcast_to(tile[None], (owners, MSG, LANES)).reshape(owners * MSG, LANES)
    tiles[pl.ds(WANT_ROW, owners, stride=MSG), :] = wanted
    message[...] = tiles[...].reshape(owners, MSG, LANES).astype(BF16)


def rank_kernel(chunk, got, items, weights, bias, out_weight, logits, tiles, first, rounded, state):
    sources = got.shape[0]
    rows = chunk * sources
    width = state.shape[1]
    layers = weights.shape[0]
    d_user = 2 * LANES
    tiles[...] = got[...].astype(F32).reshape(sources * MSG, LANES)
    wanted = tiles[pl.ds(WANT_ROW, sources, stride=MSG), :]
    people = jnp.concatenate(
        [tiles[pl.ds(USER_ROW + i, sources, stride=MSG), :] for i in range(2)], axis=1
    ).astype(BF16)
    lane = iota((sources, LANES), 1)
    high_lane = (lane >= HALF) & (wanted > 0.0)
    most = jnp.max(jnp.where(high_lane, lane - HALF + 1, 0))
    reqs = lax.axis_size("req")
    logits[...] = jnp.zeros(logits.shape, F32)

    def step(t, carry):
        lows, highs = [], []
        for k in range(chunk):
            j = t * chunk + k
            lows.append(lane_sum(jnp.where(lane == j, wanted, 0.0)))
            highs.append(lane_sum(jnp.where(lane == j + HALF, wanted, 0.0)))
        low = jnp.concatenate(lows, axis=0).astype(I32)
        high = jnp.concatenate(highs, axis=0).astype(I32)
        within = low + 256 * (high & 3)
        source = iota((rows, 1), 0) % sources
        person = ((high >> 2) & 31) * reqs + source % reqs
        pick_user = as_bf16(person == iota((rows, sources), 1))
        pick_item = as_bf16(within == iota((rows, items.shape[0]), 1))
        first[:, :d_user] = dot(pick_user, people).astype(BF16)
        first[:, d_user:] = dot(pick_item, items[...]).astype(BF16)
        state[...] = first[...].astype(F32)
        rounded[...] = first[...]

        def layer(l, carry):
            product = dot(rounded[...], weights[l]) + bias[pl.ds(l, 1), :]
            new = first[...].astype(F32) * product + state[...]
            state[...] = new
            rounded[...] = new.astype(BF16)
            return carry

        lax.fori_loop(0, layers, layer, 0)
        value = lane_sum(state[...] * out_weight[...])
        for k in range(chunk):
            j = t * chunk + k
            mine = value[k * sources : (k + 1) * sources]
            logits[...] += jnp.where(lane == j, mine, 0.0).reshape(logits.shape)
        return carry

    lax.fori_loop(0, (most + chunk - 1) // chunk, step, 0)


def score_kernel(block, got, user, codes, scores, tiles, tables):
    sources = got.shape[0]
    requests = user.shape[0]
    subs, count = codes.shape
    tiles[...] = got[...].astype(F32).reshape(sources * MSG, LANES)
    book = [tiles[pl.ds(i, sources, stride=MSG), :].astype(BF16) for i in range(CB_ROWS)]
    even = jnp.concatenate(book[:2], axis=1)
    odd = jnp.concatenate(book[2:], axis=1)
    d_user = user.shape[1]
    column = iota((d_user, sources), 0)
    people = user[...]
    of_even = dot(people, as_bf16(column == 2 * iota((d_user, sources), 1))).astype(BF16)
    of_odd = dot(people, as_bf16(column == 2 * iota((d_user, sources), 1) + 1)).astype(BF16)
    per_sub = sources // subs
    for m in range(subs):
        mine = iota((requests, sources), 1) // per_sub == m
        zero = jnp.zeros((), BF16)
        table = dot(jnp.where(mine, of_even, zero), even) + dot(jnp.where(mine, of_odd, zero), odd)
        tables[:, m * 256 : (m + 1) * 256] = table.astype(BF16)

    code = lax.broadcasted_iota(jnp.int16, (256, block), 0)

    def step(j, carry):
        at = pl.ds(pl.multiple_of(j * block, block), block)
        total = jnp.zeros((requests, block), F32)
        for m in range(subs):
            now = jnp.broadcast_to(codes[m : m + 1, at], (16, block)).astype(jnp.int16)
            now = jnp.concatenate([now] * 16, axis=0)
            onehot = jnp.where(code == now, jnp.ones((), BF16), jnp.zeros((), BF16))
            total = total + dot(tables[:, m * 256 : (m + 1) * 256], onehot)
        scores[:, at] = total
        return carry

    lax.fori_loop(0, count // block, step, 0)


def collect_kernel(back, meta, logits):
    cand_dev, requests = logits.shape
    total = meta.shape[0]
    owners = back.shape[0]
    lane = iota((total, owners), 1)
    answers = back[...].reshape(owners, LANES)
    pick = as_bf16(meta[:, 0:1] == lane)
    top = answers.astype(BF16)
    rest = answers - top.astype(F32)
    middle = rest.astype(BF16)
    last = (rest - middle.astype(F32)).astype(BF16)
    rows = dot(pick, top) + dot(pick, middle) + dot(pick, last)
    value = lane_sum(jnp.where(meta[:, 1:2] == lane, rows, 0.0))
    diagonal = iota((total, requests), 0) % requests == iota((total, requests), 1)
    spread = jnp.where(diagonal, value, 0.0)
    logits[...] = jnp.sum(spread.reshape(cand_dev, requests, requests), axis=1)


def on_device(
    user_emb,
    codebooks,
    item_codes,
    item_place,
    candidates,
    item_features,
    cross_weights,
    cross_bias,
    out_weight,
):
    requests, d_user = user_emb.shape
    cand_dev = candidates.shape[1]
    total = requests * cand_dev
    owners = lax.axis_size("item") * lax.axis_size("req")
    items = item_codes.shape[0]
    layers, width, _ = cross_weights.shape
    limit = pltpu.CompilerParams(vmem_limit_bytes=48 << 20)
    message, meta = pl.pallas_call(
        prepare_kernel,
        out_shape=(
            jax.ShapeDtypeStruct((owners, MSG, LANES), BF16),
            jax.ShapeDtypeStruct((total, LANES), I32),
        ),
        in_specs=[VMEM] * 4,
        out_specs=(VMEM, VMEM),
        scratch_shapes=[pltpu.VMEM((owners * MSG, LANES), F32)],
        compiler_params=limit,
        name="prepare",
    )(
        candidates.T,
        item_place.reshape(-1, LANES),
        jnp.swapaxes(codebooks, 1, 2)[0],
        user_emb,
    )
    got = lax.all_to_all(message, ("item", "req"), split_axis=0, concat_axis=0, tiled=True)
    chunk = 2
    rows = chunk * owners
    answers = pl.pallas_call(
        functools.partial(rank_kernel, chunk),
        out_shape=jax.ShapeDtypeStruct((owners, 1, LANES), F32),
        in_specs=[VMEM] * 5,
        out_specs=VMEM,
        scratch_shapes=[
            pltpu.VMEM((owners * MSG, LANES), F32),
            pltpu.VMEM((rows, width), BF16),
            pltpu.VMEM((rows, width), BF16),
            pltpu.VMEM((rows, width), F32),
        ],
        compiler_params=limit,
        name="rank",
    )(got, item_features, cross_weights, cross_bias, out_weight.reshape(1, width))
    back = lax.all_to_all(answers, ("item", "req"), split_axis=0, concat_axis=0, tiled=True)
    scores = pl.pallas_call(
        functools.partial(score_kernel, 512),
        out_shape=jax.ShapeDtypeStruct((requests, items), F32),
        in_specs=[VMEM] * 3,
        out_specs=VMEM,
        scratch_shapes=[
            pltpu.VMEM((owners * MSG, LANES), F32),
            pltpu.VMEM((requests, item_codes.shape[1] * 256), BF16),
        ],
        compiler_params=limit,
        name="scores",
        cost_estimate=pl.CostEstimate(flops=2 << 30, bytes_accessed=40 << 20, transcendentals=0),
    )(got, user_emb, item_codes.T)
    logits = pl.pallas_call(
        collect_kernel,
        out_shape=jax.ShapeDtypeStruct((cand_dev, requests), F32),
        in_specs=[VMEM] * 2,
        out_specs=VMEM,
        compiler_params=limit,
        name="collect",
    )(back, meta)
    return scores, logits.T


def solution(mesh):
    placed = (
        P("req", None),
        P("item", None, None),
        P("item", None),
        P(),
        P("req", "item"),
        P(("item", "req"), None),
        P(),
        P(),
        P(),
    )
    return jax.shard_map(
        on_device,
        mesh=mesh,
        in_specs=placed,
        out_specs=(P("req", "item"), P("req", "item")),
        check_vma=False,
    )
```

time: 163 us -> 76.9 us (0.47)
  matrix products: 56.4 us -> 0 us
  local copies, waits for them, and re-layouts: 56.4 us -> 5.95 us
  Pallas kernels: 0 us -> 33 us
  starting transfers between devices: 19 us -> 14.4 us
  other arithmetic: 3.91 us -> 0 us
  blocking collectives: 25.8 us -> 22.4 us
    dot_general x13 -> x0, matrix products: 56.4 us -> none  [the longest x8 47 us: score_tables(): jnp.einsum('rmk,imk->ri', tables[:, group:group + width], onehot, preferr...]
    pallas_call x0 -> x4, Pallas kernels: none -> 33 us  [the longest x1 16.3 us: on_device(): pl.pallas_call(functools.partial(rank_kernel, chunk), out_shape=jax.Shape...]
    all_gather x1 -> x0, blocking collectives: 25.8 us -> none  [on_device(): lax.all_gather(tables, 'item', axis=1, tiled=True)]
    scatter x1 -> x0, local copies, waits for them, and re-layouts: 24.6 us -> none  [on_device(): jnp.zeros((owners, capacity), jnp.int32).at[owner, ranks].set(within)]
    gather x4 -> x0, local copies, waits for them, and re-layouts: 24.4 us -> none  [the longest x2 10.5 us: on_device(): jnp.take(item_features, lax.all_to_all(wanted, ('item', 'req'), split_axi...]
    all_to_all x0 -> x1, blocking collectives: none -> 22.4 us  [on_device(): lax.all_to_all(message, ('item', 'req'), split_axis=0, concat_axis=0, til...]
    all_to_all x3 -> x0, local copies, waits for them, and re-layouts: 4.86 us -> none  [the longest x1 4.06 us: on_device(): lax.all_to_all(found, ('item', 'req'), split_axis=0, concat_axis=0, tiled...]
    all_to_all x2 -> x1, starting transfers between devices: 19 us -> 14.4 us  [on_device(): lax.all_to_all(answers, ('item', 'req'), split_axis=0, concat_axis=0, til...]
  transfers between devices with their start and end apart: 2 -> 1, of which waited for: 0 -> 0; matrix products, arithmetic and copies ran while one was open for 29% -> 0% of each run, Pallas kernels for 0% -> 18%
where the time goes in v1:
time: 76.9 us; the launch traced here: 76.5 us
  Pallas kernels  33 us (43%)
  blocking collectives  22.4 us (29%)
  starting transfers between devices  14.4 us (19%)
  local copies, waits for them, and re-layouts  5.95 us (8%)
    all_to_all x1, blocking collectives, on_device(): lax.all_to_all(message, ('item', 'req'), split_axis=0, concat_axis=0, til...  22.4 us
    pallas_call x1, Pallas kernels, on_device(): pl.pallas_call(functools.partial(rank_kernel, chunk), out_shape=jax.Shape...  16.3 us
    all_to_all x1, starting transfers between devices, on_device(): lax.all_to_all(answers, ('item', 'req'), split_axis=0, concat_axis=0, til...  14.4 us
    pallas_call x1, Pallas kernels, on_device(): pl.pallas_call(functools.partial(score_kernel, 512), out_shape=jax.ShapeD...  13.9 us
    unnamed x18, local copies, waits for them, and re-layouts  5.95 us
    pallas_call x1, Pallas kernels, on_device(): pl.pallas_call(prepare_kernel, out_shape=(jax.ShapeDtypeStruct((owners, M...  1.59 us
  transfers between devices with their start and end apart: 1, of which 0 were waited for; matrix products, arithmetic and copies ran while one was open for 0% of the time, Pallas kernels for 18%

profile of v1, /device:TPU:1, one launch (start us, length us, event | category | flops | bytes accessed | tf_op | source)
XLA Modules:
  0.0 76.5 jit_solution(13453490976250535061)
XLA Ops:
  0.6 0.0 copy-start.1
  0.6 1.0 %copy-done.1 = s32[131072]{0:T(1024)S(1)} copy-done((s32[131072]{0:T(1024)S(1)}, s32[131072]{0:T(1024)}, u32[]{:S(2)}) %copy-start.1) | copy-done | bytes 524312
  1.7 0.0 copy-start.3
  1.7 0.7 copy-done.3
  2.4 0.0 copy-start.5
  2.4 0.7 copy-done.5
  3.1 0.0 copy-start.6
  3.1 0.7 copy-done.6
  3.8 0.0 copy-start.4
  3.8 0.0 copy-start.8
  3.8 1.6 %prepare.1 = (bf16[128,8,128]{2,1,0:T(8,128)(2,1)S(1)}, s32[512,128]{1,0:T(8,128)S(1)}) custom-call(s32[16,32]{1,0:T(8,128)S(1)} %bitcast.9, s32[1024,128]{1,0:T(8,128)S(1)} %bitcast.8, bf16[8,256]{1,0:T(8,128)(2,1)S(1)} %bitcast.10, bf16[32,256]{1,0:T(8,128)(2,1)S(1)} %copy-done.3), custom_call_target="tpu_custom_call" | custom-call | tf_op jit(solution)/shard_map/prepare/pallas_call | solution.py:228
  5.4 22.4 %all_to_all.10.got = bf16[128,8,128]{2,1,0:T(8,128)(2,1)S(1)} all-to-all(bf16[128,8,128]{2,1,0:T(8,128)(2,1)S(1)} %get-tuple-element.4), channel_id=1, replica_groups=mesh['item'=32,'req'=4] {'item','req'}, dimensions={0} | all-to-all | bytes 524288 | tf_op jit(solution)/shard_map/all_to_all | solution.py:245
  27.8 0.0 copy-start
  27.8 1.4 %copy-done = bf16[1024,768]{1,0:T(8,128)(2,1)S(1)} copy-done((bf16[1024,768]{1,0:T(8,128)(2,1)S(1)}, bf16[1024,768]{1,0:T(8,128)(2,1)}, u32[]{:S(2)}) %copy-start) | copy-done | bytes 1572888
  29.2 0.0 copy-start.2
  29.2 0.7 copy-done.2
  29.9 0.7 copy-done.7
  30.6 16.3 %rank.1 = f32[128,1,128]{2,1,0:T(1,128)} custom-call(bf16[128,8,128]{2,1,0:T(8,128)(2,1)S(1)} %all_to_all.10.got, bf16[1024,768]{1,0:T(8,128)(2,1)S(1)} %copy-done, bf16[4,1024,1024]{2,1,0:T(8,128)(2,1)} %weights.1, f32[4,1024]{1,0:T(4,128)S(1)} %copy-done.2, f32[1,1024]{1,0:T(1,128)S(1)} %bitcast.11), custom_call_target="tpu_custom_call" | custom-call | tf_op jit(solution)/shard_map/rank/pallas_call | solution.py:248
  47.0 14.4 %all-to-all-start.1 = ((f32[128,1,128]{2,1,0:T(1,128)}), f32[128,1,128]{2,1,0:T(1,128)S(1)}, u32[]{:S(2)}, u32[]{:S(2)}) async-start(f32[128,1,128]{2,1,0:T(1,128)} %rank.1), calls=%async_computation.1 | async-start | bytes 131072 | tf_op jit(solution)/shard_map/all_to_all | solution.py:262
  61.4 0.0 copy-done.4
  61.4 0.0 copy-done.8
  61.4 13.9 %scores.1 = f32[32,4096]{1,0:T(8,128)} custom-call(bf16[128,8,128]{2,1,0:T(8,128)(2,1)S(1)} %all_to_all.10.got, bf16[32,256]{1,0:T(8,128)(2,1)S(1)} %copy-done.4, s32[32,4096]{1,0:T(8,128)S(1)} %bitcast.12), custom_call_target="tpu_custom_call" | custom-call | flops 2147483648 | bytes 41943040 | tf_op jit(solution)/shard_map/scores/pallas_call | solution.py:263
  75.3 0.0 all-to-all-done.1.back
  75.3 1.2 %collect.1 = f32[16,32]{1,0:T(8,128)} custom-call(f32[128,1,128]{2,1,0:T(1,128)S(1)} %all-to-all-done.1.back, s32[512,128]{1,0:T(8,128)S(1)} %get-tuple-element.5.meta), custom_call_target="tpu_custom_call" | custom-call | tf_op jit(solution)/shard_map/collect/pallas_call | solution.py:276
  (1 shorter events, 0.0 us)
Async XLA Ops:
  0.6 1.0 %copy-start.1 = (s32[131072]{0:T(1024)S(1)}, s32[131072]{0:T(1024)}, u32[]{:S(2)}) copy-start(s32[131072]{0:T(1024)} %param.12) | copy-start | bytes 1572868
  1.7 0.7 copy-start.3
  2.4 0.7 copy-start.5
  3.1 0.7 copy-start.6
  3.8 57.6 %copy-start.4 = (bf16[32,256]{1,0:T(8,128)(2,1)S(1)}, bf16[32,256]{1,0:T(8,128)(2,1)}, u32[]{:S(2)}) copy-start(bf16[32,256]{1,0:T(8,128)(2,1)} %user.3) | copy-start | bytes 49156
  3.8 57.6 %copy-start.8 = (s32[4096,32]{0,1:T(8,128)S(1)}, s32[4096,32]{0,1:T(8,128)}, u32[]{:S(2)}) copy-start(s32[4096,32]{0,1:T(8,128)} %param.11) | copy-start | bytes 1572868
  27.8 1.4 %copy-start = (bf16[1024,768]{1,0:T(8,128)(2,1)S(1)}, bf16[1024,768]{1,0:T(8,128)(2,1)}, u32[]{:S(2)}) copy-start(bf16[1024,768]{1,0:T(8,128)(2,1)} %items.1) | copy-start | bytes 4718596
  29.2 0.7 copy-start.2
  29.9 0.7 copy-start.7
  47.0 28.3 %all-to-all-start.1 = ((f32[128,1,128]{2,1,0:T(1,128)}), f32[128,1,128]{2,1,0:T(1,128)S(1)}, u32[]{:S(2)}, u32[]{:S(2)}) async-start(f32[128,1,128]{2,1,0:T(1,128)} %rank.1), calls=%async_computation.1 | async-start | bytes 131072 | tf_op jit(solution)/shard_map/all_to_all | solution.py:262

commit v2 on v1

--- a/solution.py
+++ b/solution.py
@@ -10,6 +10,7 @@
 F32 = jnp.float32
 BF16 = jnp.bfloat16
 I32 = jnp.int32
+HBM = pl.BlockSpec(memory_space=pltpu.HBM)
 VMEM = pl.BlockSpec(memory_space=pltpu.VMEM)
 LANES = 128
 MSG = 8
@@ -35,7 +36,15 @@
     return jnp.where(mask, 1.0, 0.0).astype(BF16)
 
 
-def prepare_kernel(cand, place, codebook, user, message, meta, tiles):
+def prepare_kernel(
+    cand_in, place_in, codebook_in, user_in, message, meta, tiles, cand, place, codebook, user, sems
+):
+    pairs = ((cand_in, cand), (place_in, place), (codebook_in, codebook), (user_in, user))
+    copies = [pltpu.make_async_copy(a, b, sems.at[i]) for i, (a, b) in enumerate(pairs)]
+    for copy in copies:
+        copy.start()
+    for copy in copies:
+        copy.wait()
     cand_dev, requests = cand.shape
     total = cand_dev * requests
     owners = message.shape[0]
@@ -100,12 +109,40 @@
     message[...] = tiles[...].reshape(owners, MSG, LANES).astype(BF16)
 
 
-def rank_kernel(chunk, got, items, weights, bias, out_weight, logits, tiles, first, rounded, state):
+def rank_kernel(
+    chunk,
+    block,
+    got_in,
+    items_in,
+    weights_in,
+    bias_in,
+    out_weight_in,
+    logits,
+    got,
+    items,
+    weights,
+    bias,
+    out_weight,
+    tiles,
+    first,
+    rounded,
+    state,
+    sems,
+):
+    pairs = [(got_in, got), (items_in, items), (bias_in, bias), (out_weight_in, out_weight)]
+    pairs += [(weights_in.at[i], weights.at[i]) for i in range(weights.shape[0])]
+    copies = [pltpu.make_async_copy(a, b, sems.at[i]) for i, (a, b) in enumerate(pairs)]
+    for copy in copies:
+        copy.start()
+    copies[0].wait()
     sources = got.shape[0]
-    rows = chunk * sources
+    halves = 2
+    per = chunk // halves
+    rows = per * sources
     width = state.shape[1]
     layers = weights.shape[0]
-    d_user = 2 * LANES
+    features = items.shape[1]
+    d_user = width - features
     tiles[...] = got[...].astype(F32).reshape(sources * MSG, LANES)
     wanted = tiles[pl.ds(WANT_ROW, sources, stride=MSG), :]
     people = jnp.concatenate(
@@ -116,41 +153,62 @@
     most = jnp.max(jnp.where(high_lane, lane - HALF + 1, 0))
     reqs = lax.axis_size("req")
     logits[...] = jnp.zeros(logits.shape, F32)
+    source = iota((rows, 1), 0) % sources
+
+    def arrive(t, some):
+        @pl.when(t == 0)
+        def _():
+            for copy in some:
+                copy.wait()
 
     def step(t, carry):
-        lows, highs = [], []
-        for k in range(chunk):
-            j = t * chunk + k
-            lows.append(lane_sum(jnp.where(lane == j, wanted, 0.0)))
-            highs.append(lane_sum(jnp.where(lane == j + HALF, wanted, 0.0)))
-        low = jnp.concatenate(lows, axis=0).astype(I32)
-        high = jnp.concatenate(highs, axis=0).astype(I32)
-        within = low + 256 * (high & 3)
-        source = iota((rows, 1), 0) % sources
-        person = ((high >> 2) & 31) * reqs + source % reqs
-        pick_user = as_bf16(person == iota((rows, sources), 1))
-        pick_item = as_bf16(within == iota((rows, items.shape[0]), 1))
-        first[:, :d_user] = dot(pick_user, people).astype(BF16)
-        first[:, d_user:] = dot(pick_item, items[...]).astype(BF16)
-        state[...] = first[...].astype(F32)
-        rounded[...] = first[...]
-
-        def layer(l, carry):
-            product = dot(rounded[...], weights[l]) + bias[pl.ds(l, 1), :]
-            new = first[...].astype(F32) * product + state[...]
-            state[...] = new
-            rounded[...] = new.astype(BF16)
-            return carry
-
-        lax.fori_loop(0, layers, layer, 0)
-        value = lane_sum(state[...] * out_weight[...])
-        for k in range(chunk):
-            j = t * chunk + k
-            mine = value[k * sources : (k + 1) * sources]
-            logits[...] += jnp.where(lane == j, mine, 0.0).reshape(logits.shape)
+        arrive(t, copies[1:4])
+        for h in range(halves):
+            at = slice(h * rows, (h + 1) * rows)
+            lows, highs = [], []
+            for k in range(per):
+                j = t * chunk + h * per + k
+                lows.append(lane_sum(jnp.where(lane == j, wanted, 0.0)))
+                highs.append(lane_sum(jnp.where(lane == j + HALF, wanted, 0.0)))
+            low = jnp.concatenate(lows, axis=0).astype(I32)
+            high = jnp.concatenate(highs, axis=0).astype(I32)
+            within = low + 256 * (high & 3)
+            person = ((high >> 2) & 31) * reqs + source % reqs
+            pick_user = as_bf16(person == iota((rows, sources), 1))
+            pick_item = as_bf16(within == iota((rows, items.shape[0]), 1))
+            first[at, :d_user] = dot(pick_user, people).astype(BF16)
+            for n in range(0, features, block):
+                first[at, d_user + n : d_user + n + block] = dot(
+                    pick_item, items[:, n : n + block]
+                ).astype(BF16)
+        parts = [jnp.zeros((rows, LANES), F32) for _ in range(halves)]
+        for layer in range(layers):
+            if layer < 2:
+                arrive(t, copies[4:5] if layer == 0 else copies[5:])
+            for h in range(halves):
+                at = slice(h * rows, (h + 1) * rows)
+                left = first[at, :] if layer == 0 else rounded[(layer + 1) % 2, at, :]
+                for n in range(0, width, block):
+                    to = slice(n, n + block)
+                    product = dot(left, weights[layer, :, to]) + bias[layer : layer + 1, to]
+                    start = first[at, to].astype(F32)
+                    new = start * product + (start if layer == 0 else state[at, to])
+                    if layer < layers - 1:
+                        state[at, to] = new
+                        rounded[layer % 2, at, to] = new.astype(BF16)
+                    else:
+                        new = new * out_weight[:, to]
+                        for i in range(0, block, LANES):
+                            parts[h] = parts[h] + new[:, i : i + LANES]
+        for h in range(halves):
+            value = lane_sum(parts[h])
+            for k in range(per):
+                j = t * chunk + h * per + k
+                mine = value[k * sources : (k + 1) * sources]
+                logits[...] += jnp.where(lane == j, mine, 0.0).reshape(logits.shape)
         return carry
 
-    lax.fori_loop(0, (most + chunk - 1) // chunk, step, 0)
+    lax.fori_loop(0, jnp.maximum((most + chunk - 1) // chunk, 1), step, 0)
 
 
 def score_kernel(block, got, user, codes, scores, tiles, tables):
@@ -224,17 +282,25 @@
     owners = lax.axis_size("item") * lax.axis_size("req")
     items = item_codes.shape[0]
     layers, width, _ = cross_weights.shape
-    limit = pltpu.CompilerParams(vmem_limit_bytes=48 << 20)
+    whole = pltpu.CompilerParams(vmem_limit_bytes=60 << 20)
+    limit = pltpu.CompilerParams(vmem_limit_bytes=24 << 20)
     message, meta = pl.pallas_call(
         prepare_kernel,
         out_shape=(
             jax.ShapeDtypeStruct((owners, MSG, LANES), BF16),
             jax.ShapeDtypeStruct((total, LANES), I32),
         ),
-        in_specs=[VMEM] * 4,
+        in_specs=[HBM] * 4,
         out_specs=(VMEM, VMEM),
-        scratch_shapes=[pltpu.VMEM((owners * MSG, LANES), F32)],
-        compiler_params=limit,
+        scratch_shapes=[
+            pltpu.VMEM((owners * MSG, LANES), F32),
+            pltpu.VMEM((cand_dev, requests), I32),
+            pltpu.VMEM((item_place.shape[0] // LANES, LANES), I32),
+            pltpu.VMEM(codebooks.shape[:0:-1], BF16),
+            pltpu.VMEM(user_emb.shape, BF16),
+            pltpu.SemaphoreType.DMA((4,)),
+        ],
+        compiler_params=whole,
         name="prepare",
     )(
         candidates.T,
@@ -243,21 +309,28 @@
         user_emb,
     )
     got = lax.all_to_all(message, ("item", "req"), split_axis=0, concat_axis=0, tiled=True)
-    chunk = 2
+    chunk = 4
     rows = chunk * owners
     answers = pl.pallas_call(
-        functools.partial(rank_kernel, chunk),
+        functools.partial(rank_kernel, chunk, 256),
         out_shape=jax.ShapeDtypeStruct((owners, 1, LANES), F32),
-        in_specs=[VMEM] * 5,
+        in_specs=[HBM] * 5,
         out_specs=VMEM,
         scratch_shapes=[
+            pltpu.VMEM((owners, MSG, LANES), BF16),
+            pltpu.VMEM(item_features.shape, BF16),
+            pltpu.VMEM(cross_weights.shape, BF16),
+            pltpu.VMEM(cross_bias.shape, F32),
+            pltpu.VMEM((1, width), F32),
             pltpu.VMEM((owners * MSG, LANES), F32),
             pltpu.VMEM((rows, width), BF16),
-            pltpu.VMEM((rows, width), BF16),
+            pltpu.VMEM((2, rows, width), BF16),
             pltpu.VMEM((rows, width), F32),
-        ],
-        compiler_params=limit,
+            pltpu.SemaphoreType.DMA((4 + layers,)),
+        ],
+        compiler_params=whole,
         name="rank",
+        cost_estimate=pl.CostEstimate(flops=12 << 30, bytes_accessed=10 << 20, transcendentals=0),
     )(got, item_features, cross_weights, cross_bias, out_weight.reshape(1, width))
     back = lax.all_to_all(answers, ("item", "req"), split_axis=0, concat_axis=0, tiled=True)
     scores = pl.pallas_call(

time: 76.9 us -> 67.4 us (0.88); the launches traced: 76.5 us -> 68.3 us
  local copies, waits for them, and re-layouts: 5.95 us -> 0.01 us
  starting transfers between devices: 14.4 us -> 10.6 us
  Pallas kernels: 33 us -> 34.3 us
    unnamed x18 -> x8, local copies, waits for them, and re-layouts: 5.95 us -> 0.01 us
    all_to_all x1, starting transfers between devices: 14.4 us -> 10.6 us  [on_device(): lax.all_to_all(answers, ('item', 'req'), split_axis=0, concat_axis=0, til...]
    pallas_call x1, Pallas kernels: 1.59 us -> 3.39 us  [on_device(): pl.pallas_call(prepare_kernel, out_shape=(jax.ShapeDtypeStruct((owners, M...]
  transfers between devices with their start and end apart: 1 -> 1, of which waited for: 0 -> 0; matrix products, arithmetic and copies ran while one was open for 0% -> 0% of each run, Pallas kernels for 18% -> 20%
where the time goes in v2:
time: 67.4 us; the launch traced here: 68.3 us
  Pallas kernels  34.3 us (51%)
  blocking collectives  22.7 us (34%)
  starting transfers between devices  10.6 us (16%)
  between operations  0.68 us (1%)
    all_to_all x1, blocking collectives, on_device(): lax.all_to_all(message, ('item', 'req'), split_axis=0, concat_axis=0, til...  22.7 us
    pallas_call x1, Pallas kernels, on_device(): pl.pallas_call(functools.partial(rank_kernel, chunk, 256), out_shape=jax....  15.8 us
    pallas_call x1, Pallas kernels, on_device(): pl.pallas_call(functools.partial(score_kernel, 512), out_shape=jax.ShapeD...  13.9 us
    all_to_all x1, starting transfers between devices, on_device(): lax.all_to_all(answers, ('item', 'req'), split_axis=0, concat_axis=0, til...  10.6 us
    pallas_call x1, Pallas kernels, on_device(): pl.pallas_call(prepare_kernel, out_shape=(jax.ShapeDtypeStruct((owners, M...  3.39 us
  transfers between devices with their start and end apart: 1, of which 0 were waited for; matrix products, arithmetic and copies ran while one was open for 0% of the time, Pallas kernels for 20%

profile of v2, /device:TPU:1, one launch (start us, length us, event | category | flops | bytes accessed | tf_op | source)
XLA Modules:
  0.0 68.3 jit_solution(4047499543023547696)
XLA Ops:
  0.6 3.4 %prepare.1 = (bf16[128,8,128]{2,1,0:T(8,128)(2,1)}, s32[512,128]{1,0:T(8,128)}) custom-call(s32[16,32]{1,0:T(8,128)} %bitcast.10, s32[1024,128]{1,0:T(8,128)} %bitcast.9, bf16[8,256]{1,0:T(8,128)(2,1)} %bitcast.12, bf16[32,256]{1,0:T(8,128)(2,1)} %user.1), custom_call_target="tpu_custom_call" | custom-call | tf_op jit(solution)/shard_map/prepare/pallas_call | solution.py:287
  4.0 22.7 %all_to_all.10.got.got_in = bf16[128,8,128]{2,1,0:T(8,128)(2,1)} all-to-all(bf16[128,8,128]{2,1,0:T(8,128)(2,1)} %get-tuple-element.4), channel_id=1, replica_groups=mesh['item'=32,'req'=4] {'item','req'}, dimensions={0} | all-to-all | bytes 524288 | tf_op jit(solution)/shard_map/all_to_all | solution.py:311
  26.8 0.0 copy-start.1
  26.8 0.0 copy-start.2
  26.8 0.0 copy-start.3
  26.8 0.0 copy-start
  26.8 15.8 %rank.1 = f32[128,1,128]{2,1,0:T(1,128)} custom-call(bf16[128,8,128]{2,1,0:T(8,128)(2,1)} %all_to_all.10.got.got_in, bf16[1024,768]{1,0:T(8,128)(2,1)} %items_in.1, bf16[4,1024,1024]{2,1,0:T(8,128)(2,1)} %weights_in.1, f32[4,1024]{1,0:T(4,128)} %bias_in.1, f32[1,1024]{1,0:T(1,128)} %bitcast.13), custom_call_target="tpu_custom_call" | custom-call | flops 12884901888 | bytes 10485760 | tf_op jit(solution)/shard_map/rank/pallas_call | solution.py:314
  42.6 10.6 %all-to-all-start.1 = ((f32[128,1,128]{2,1,0:T(1,128)}), f32[128,1,128]{2,1,0:T(1,128)S(1)}, u32[]{:S(2)}, u32[]{:S(2)}) async-start(f32[128,1,128]{2,1,0:T(1,128)} %rank.1), calls=%async_computation.1 | async-start | bytes 131072 | tf_op jit(solution)/shard_map/all_to_all | solution.py:335
  53.2 0.0 copy-done.1
  53.2 0.0 copy-done.2
  53.2 0.0 copy-done.3
  53.2 13.9 %scores.1 = f32[32,4096]{1,0:T(8,128)} custom-call(bf16[128,8,128]{2,1,0:T(8,128)(2,1)S(1)} %copy-done.1, bf16[32,256]{1,0:T(8,128)(2,1)S(1)} %copy-done.2, s32[32,4096]{1,0:T(8,128)S(1)} %bitcast.8), custom_call_target="tpu_custom_call" | custom-call | flops 2147483648 | bytes 41943040 | tf_op jit(solution)/shard_map/scores/pallas_call | solution.py:336
  67.1 0.0 all-to-all-done.1.back
  67.1 0.0 copy-done
  67.1 1.2 %collect.1 = f32[16,32]{1,0:T(8,128)} custom-call(f32[128,1,128]{2,1,0:T(1,128)S(1)} %all-to-all-done.1.back, s32[512,128]{1,0:T(8,128)S(1)} %copy-done), custom_call_target="tpu_custom_call" | custom-call | tf_op jit(solution)/shard_map/collect/pallas_call | solution.py:349
Async XLA Ops:
  26.8 26.4 %copy-start.1 = (bf16[128,8,128]{2,1,0:T(8,128)(2,1)S(1)}, bf16[128,8,128]{2,1,0:T(8,128)(2,1)}, u32[]{:S(2)}) copy-start(bf16[128,8,128]{2,1,0:T(8,128)(2,1)} %all_to_all.10.got.got_in) | copy-start | bytes 786436
  26.8 26.4 %copy-start.2 = (bf16[32,256]{1,0:T(8,128)(2,1)S(1)}, bf16[32,256]{1,0:T(8,128)(2,1)}, u32[]{:S(2)}) copy-start(bf16[32,256]{1,0:T(8,128)(2,1)} %user.1) | copy-start | bytes 49156
  26.8 26.5 %copy-start.3 = (s32[4096,32]{0,1:T(8,128)S(1)}, s32[4096,32]{0,1:T(8,128)}, u32[]{:S(2)}) copy-start(s32[4096,32]{0,1:T(8,128)} %param.11) | copy-start | bytes 1572868
  26.8 40.4 %copy-start = (s32[512,128]{1,0:T(8,128)S(1)}, s32[512,128]{1,0:T(8,128)}, u32[]{:S(2)}) copy-start(s32[512,128]{1,0:T(8,128)} %get-tuple-element.5.meta) | copy-start | bytes 786436
  42.6 24.5 %all-to-all-start.1 = ((f32[128,1,128]{2,1,0:T(1,128)}), f32[128,1,128]{2,1,0:T(1,128)S(1)}, u32[]{:S(2)}, u32[]{:S(2)}) async-start(f32[128,1,128]{2,1,0:T(1,128)} %rank.1), calls=%async_computation.1 | async-start | bytes 131072 | tf_op jit(solution)/shard_map/all_to_all | solution.py:335

commit v3 on v2

--- a/solution.py
+++ b/solution.py
@@ -18,6 +18,7 @@
 USER_ROW = 4
 WANT_ROW = 6
 HALF = 64
+CODES = 256
 
 
 def dot(a, b, dims=(((1,), (0,)), ((), ()))):
@@ -127,6 +128,7 @@
     first,
     rounded,
     state,
+    answer,
     sems,
 ):
     pairs = [(got_in, got), (items_in, items), (bias_in, bias), (out_weight_in, out_weight)]
@@ -152,7 +154,7 @@
     high_lane = (lane >= HALF) & (wanted > 0.0)
     most = jnp.max(jnp.where(high_lane, lane - HALF + 1, 0))
     reqs = lax.axis_size("req")
-    logits[...] = jnp.zeros(logits.shape, F32)
+    answer[...] = jnp.zeros(answer.shape, F32)
     source = iota((rows, 1), 0) % sources
 
     def arrive(t, some):
@@ -205,43 +207,69 @@
             for k in range(per):
                 j = t * chunk + h * per + k
                 mine = value[k * sources : (k + 1) * sources]
-                logits[...] += jnp.where(lane == j, mine, 0.0).reshape(logits.shape)
+                answer[...] += jnp.where(lane == j, mine, 0.0)
         return carry
 
     lax.fori_loop(0, jnp.maximum((most + chunk - 1) // chunk, 1), step, 0)
-
-
-def score_kernel(block, got, user, codes, scores, tiles, tables):
+    logits[...] = answer[...].reshape(logits.shape)
+
+
+def score_kernel(block, looked, got, user, codes, scores, tiles, tables, wide):
     sources = got.shape[0]
-    requests = user.shape[0]
+    requests, d_user = user.shape
     subs, count = codes.shape
     tiles[...] = got[...].astype(F32).reshape(sources * MSG, LANES)
     book = [tiles[pl.ds(i, sources, stride=MSG), :].astype(BF16) for i in range(CB_ROWS)]
     even = jnp.concatenate(book[:2], axis=1)
     odd = jnp.concatenate(book[2:], axis=1)
-    d_user = user.shape[1]
     column = iota((d_user, sources), 0)
     people = user[...]
     of_even = dot(people, as_bf16(column == 2 * iota((d_user, sources), 1))).astype(BF16)
     of_odd = dot(people, as_bf16(column == 2 * iota((d_user, sources), 1) + 1)).astype(BF16)
     per_sub = sources // subs
+    zero = jnp.zeros((), BF16)
     for m in range(subs):
         mine = iota((requests, sources), 1) // per_sub == m
-        zero = jnp.zeros((), BF16)
         table = dot(jnp.where(mine, of_even, zero), even) + dot(jnp.where(mine, of_odd, zero), odd)
-        tables[:, m * 256 : (m + 1) * 256] = table.astype(BF16)
-
-    code = lax.broadcasted_iota(jnp.int16, (256, block), 0)
+        table = table.astype(BF16)
+        if m < looked:
+            wide[m] = table.astype(F32)
+        else:
+            tables[:, m * CODES : (m + 1) * CODES] = table
+
+    code = lax.broadcasted_iota(jnp.int16, (CODES, block), 0)
+    one = jnp.ones((), BF16)
+    groups, spans = requests // 8, block // LANES
+    order = sorted(
+        [((i + 0.5) / looked, i) for i in range(looked)]
+        + [((i + 0.5) / (subs - looked), i + looked) for i in range(subs - looked)]
+    )
+
+    def pick(values, index):
+        return jnp.take_along_axis(values, index, axis=1, mode="promise_in_bounds")
 
     def step(j, carry):
         at = pl.ds(pl.multiple_of(j * block, block), block)
         total = jnp.zeros((requests, block), F32)
-        for m in range(subs):
-            now = jnp.broadcast_to(codes[m : m + 1, at], (16, block)).astype(jnp.int16)
-            now = jnp.concatenate([now] * 16, axis=0)
-            onehot = jnp.where(code == now, jnp.ones((), BF16), jnp.zeros((), BF16))
-            total = total + dot(tables[:, m * 256 : (m + 1) * 256], onehot)
-        scores[:, at] = total
+        sums = [[jnp.zeros((8, LANES), F32) for _ in range(spans)] for _ in range(groups)]
+        for _, m in order:
+            row = codes[m : m + 1, at]
+            if m >= looked:
+                now = jnp.broadcast_to(row, (16, block)).astype(jnp.int16)
+                now = jnp.concatenate([now] * (CODES // 16), axis=0)
+                onehot = jnp.where(code == now, one, zero)
+                total = total + dot(tables[:, m * CODES : (m + 1) * CODES], onehot)
+                continue
+            for b in range(spans):
+                now = jnp.broadcast_to(row[:, b * LANES : (b + 1) * LANES], (8, LANES))
+                index = now & (LANES - 1)
+                upper = now >= LANES
+                for g in range(groups):
+                    low = pick(wide[m, g * 8 : (g + 1) * 8, :LANES], index)
+                    high = pick(wide[m, g * 8 : (g + 1) * 8, LANES:], index)
+                    sums[g][b] = sums[g][b] + jnp.where(upper, high, low)
+        rows = [jnp.concatenate(group, axis=1) for group in sums]
+        scores[:, at] = total + jnp.concatenate(rows, axis=0)
         return carry
 
     lax.fori_loop(0, count // block, step, 0)
@@ -326,6 +354,7 @@
             pltpu.VMEM((rows, width), BF16),
             pltpu.VMEM((2, rows, width), BF16),
             pltpu.VMEM((rows, width), F32),
+            pltpu.VMEM((owners, LANES), F32),
             pltpu.SemaphoreType.DMA((4 + layers,)),
         ],
         compiler_params=whole,
@@ -333,14 +362,16 @@
         cost_estimate=pl.CostEstimate(flops=12 << 30, bytes_accessed=10 << 20, transcendentals=0),
     )(got, item_features, cross_weights, cross_bias, out_weight.reshape(1, width))
     back = lax.all_to_all(answers, ("item", "req"), split_axis=0, concat_axis=0, tiled=True)
+    looked = 14
     scores = pl.pallas_call(
-        functools.partial(score_kernel, 512),
+        functools.partial(score_kernel, 512, looked),
         out_shape=jax.ShapeDtypeStruct((requests, items), F32),
         in_specs=[VMEM] * 3,
         out_specs=VMEM,
         scratch_shapes=[
             pltpu.VMEM((owners * MSG, LANES), F32),
-            pltpu.VMEM((requests, item_codes.shape[1] * 256), BF16),
+            pltpu.VMEM((requests, item_codes.shape[1] * CODES), BF16),
+            pltpu.VMEM((looked, requests, CODES), F32),
         ],
         compiler_params=limit,
         name="scores",

time: 67.4 us -> 63 us (0.935); the launches traced: 68.3 us -> 62.5 us
  Pallas kernels: 34.3 us -> 29.4 us
  starting transfers between devices: 10.6 us -> 9.21 us
    pallas_call x1, Pallas kernels: 13.9 us -> 9.14 us  [on_device(): pl.pallas_call(functools.partial(score_kernel, 512, looked), out_shape=ja...]
    all_to_all x1, starting transfers between devices: 10.6 us -> 9.21 us  [on_device(): lax.all_to_all(answers, ('item', 'req'), split_axis=0, concat_axis=0, til...]
  transfers between devices with their start and end apart: 1 -> 1, of which waited for: 0 -> 1; matrix products, arithmetic and copies ran while one was open for 0% -> 0% of each run, Pallas kernels for 20% -> 15%
where the time goes in v3:
time: 63 us; the launch traced here: 62.5 us
  Pallas kernels  29.4 us (47%)
  blocking collectives  22.7 us (36%)
  starting transfers between devices  9.21 us (15%)
  between operations  0.68 us (1%)
    all_to_all x1, blocking collectives, on_device(): lax.all_to_all(message, ('item', 'req'), split_axis=0, concat_axis=0, til...  22.7 us
    pallas_call x1, Pallas kernels, on_device(): pl.pallas_call(functools.partial(rank_kernel, chunk, 256), out_shape=jax....  15.7 us
    all_to_all x1, starting transfers between devices, on_device(): lax.all_to_all(answers, ('item', 'req'), split_axis=0, concat_axis=0, til...  9.21 us
    pallas_call x1, Pallas kernels, on_device(): pl.pallas_call(functools.partial(score_kernel, 512, looked), out_shape=ja...  9.14 us
    pallas_call x1, Pallas kernels, on_device(): pl.pallas_call(prepare_kernel, out_shape=(jax.ShapeDtypeStruct((owners, M...  3.39 us
  transfers between devices with their start and end apart: 1, of which 1 were waited for; matrix products, arithmetic and copies ran while one was open for 0% of the time, Pallas kernels for 15%

profile of v3, /device:TPU:1, one launch (start us, length us, event | category | flops | bytes accessed | tf_op | source)
XLA Modules:
  0.0 62.5 jit_solution(17562438247212578511)
XLA Ops:
  0.6 3.4 %prepare.1 = (bf16[128,8,128]{2,1,0:T(8,128)(2,1)}, s32[512,128]{1,0:T(8,128)}) custom-call(s32[16,32]{1,0:T(8,128)} %bitcast.10, s32[1024,128]{1,0:T(8,128)} %bitcast.9, bf16[8,256]{1,0:T(8,128)(2,1)} %bitcast.12, bf16[32,256]{1,0:T(8,128)(2,1)} %user.1), custom_call_target="tpu_custom_call" | custom-call | tf_op jit(solution)/shard_map/prepare/pallas_call | solution.py:315
  4.0 22.7 %all_to_all.10.got.got_in = bf16[128,8,128]{2,1,0:T(8,128)(2,1)} all-to-all(bf16[128,8,128]{2,1,0:T(8,128)(2,1)} %get-tuple-element.4), channel_id=1, replica_groups=mesh['item'=32,'req'=4] {'item','req'}, dimensions={0} | all-to-all | bytes 524288 | tf_op jit(solution)/shard_map/all_to_all | solution.py:339
  26.8 0.0 copy-start.1
  26.8 0.0 copy-start.2
  26.8 0.0 copy-start.3
  26.8 0.0 copy-start
  26.8 15.7 %rank.1 = f32[128,1,128]{2,1,0:T(1,128)} custom-call(bf16[128,8,128]{2,1,0:T(8,128)(2,1)} %all_to_all.10.got.got_in, bf16[1024,768]{1,0:T(8,128)(2,1)} %items_in.1, bf16[4,1024,1024]{2,1,0:T(8,128)(2,1)} %weights_in.1, f32[4,1024]{1,0:T(4,128)} %bias_in.1, f32[1,1024]{1,0:T(1,128)} %bitcast.13), custom_call_target="tpu_custom_call" | custom-call | flops 12884901888 | bytes 10485760 | tf_op jit(solution)/shard_map/rank/pallas_call | solution.py:342
  42.5 9.2 %all-to-all-start.1 = ((f32[128,1,128]{2,1,0:T(1,128)}), f32[128,1,128]{2,1,0:T(1,128)S(1)}, u32[]{:S(2)}, u32[]{:S(2)}) async-start(f32[128,1,128]{2,1,0:T(1,128)} %rank.1), calls=%async_computation.1 | async-start | bytes 131072 | tf_op jit(solution)/shard_map/all_to_all | solution.py:364
  51.7 0.0 copy-done.1
  51.7 0.0 copy-done.2
  51.7 0.0 copy-done.3
  51.7 9.1 %scores.1 = f32[32,4096]{1,0:T(8,128)} custom-call(bf16[128,8,128]{2,1,0:T(8,128)(2,1)S(1)} %copy-done.1, bf16[32,256]{1,0:T(8,128)(2,1)S(1)} %copy-done.2, s32[32,4096]{1,0:T(8,128)S(1)} %bitcast.8), custom_call_target="tpu_custom_call" | custom-call | flops 2147483648 | bytes 41943040 | tf_op jit(solution)/shard_map/scores/pallas_call | solution.py:366
  60.9 0.4 all-to-all-done.1.back
  61.3 0.0 copy-done
  61.3 1.2 %collect.1 = f32[16,32]{1,0:T(8,128)} custom-call(f32[128,1,128]{2,1,0:T(1,128)S(1)} %all-to-all-done.1.back, s32[512,128]{1,0:T(8,128)S(1)} %copy-done), custom_call_target="tpu_custom_call" | custom-call | tf_op jit(solution)/shard_map/collect/pallas_call | solution.py:380
Async XLA Ops:
  26.8 24.9 %copy-start.1 = (bf16[128,8,128]{2,1,0:T(8,128)(2,1)S(1)}, bf16[128,8,128]{2,1,0:T(8,128)(2,1)}, u32[]{:S(2)}) copy-start(bf16[128,8,128]{2,1,0:T(8,128)(2,1)} %all_to_all.10.got.got_in) | copy-start | bytes 786436
  26.8 24.9 %copy-start.2 = (bf16[32,256]{1,0:T(8,128)(2,1)S(1)}, bf16[32,256]{1,0:T(8,128)(2,1)}, u32[]{:S(2)}) copy-start(bf16[32,256]{1,0:T(8,128)(2,1)} %user.1) | copy-start | bytes 49156
  26.8 25.0 %copy-start.3 = (s32[4096,32]{0,1:T(8,128)S(1)}, s32[4096,32]{0,1:T(8,128)}, u32[]{:S(2)}) copy-start(s32[4096,32]{0,1:T(8,128)} %param.11) | copy-start | bytes 1572868
  26.8 34.5 %copy-start = (s32[512,128]{1,0:T(8,128)S(1)}, s32[512,128]{1,0:T(8,128)}, u32[]{:S(2)}) copy-start(s32[512,128]{1,0:T(8,128)} %get-tuple-element.5.meta) | copy-start | bytes 786436
  42.5 18.8 %all-to-all-start.1 = ((f32[128,1,128]{2,1,0:T(1,128)}), f32[128,1,128]{2,1,0:T(1,128)S(1)}, u32[]{:S(2)}, u32[]{:S(2)}) async-start(f32[128,1,128]{2,1,0:T(1,128)} %rank.1), calls=%async_computation.1 | async-start | bytes 131072 | tf_op jit(solution)/shard_map/all_to_all | solution.py:364

commit v4 on v3

--- a/solution.py
+++ b/solution.py
@@ -110,52 +110,105 @@
     message[...] = tiles[...].reshape(owners, MSG, LANES).astype(BF16)
 
 
+def project_kernel(band, items_in, weights_in, table, items, weights, tiles, sems):
+    stored, features = items.shape
+    width = weights.shape[1]
+    d_user = width - features
+    copies = [
+        pltpu.make_async_copy(items_in, items, sems.at[0]),
+        pltpu.make_async_copy(weights_in.at[0, pl.ds(d_user, features)], weights, sems.at[1]),
+    ]
+    for copy in copies:
+        copy.start()
+    for copy in copies:
+        copy.wait()
+    chunks = width // LANES
+    lines = band * 2 * chunks
+    copies = []
+    for n in range(stored // band):
+        rows = slice(n * band, (n + 1) * band)
+        for c in range(chunks):
+            at = c * LANES - d_user
+            part = jnp.zeros((band, LANES), F32)
+            if at >= 0:
+                part = items[rows, at : at + LANES].astype(F32)
+            tiles[pl.ds(n * lines + c, band, stride=2 * chunks), :] = part
+        for c in range(0, chunks, 2):
+            product = dot(items[rows, :], weights[:, c * LANES : (c + 2) * LANES])
+            for i in range(2):
+                to = pl.ds(n * lines + chunks + c + i, band, stride=2 * chunks)
+                tiles[to, :] = product[:, i * LANES : (i + 1) * LANES]
+        whole = pl.ds(n * lines, lines)
+        copies.append(pltpu.make_async_copy(tiles.at[whole], table.at[whole], sems.at[2 + n]))
+        copies[-1].start()
+    for copy in copies:
+        copy.wait()
+
+
 def rank_kernel(
     chunk,
     block,
-    got_in,
-    items_in,
+    stretch,
+    got,
+    table_in,
     weights_in,
-    bias_in,
-    out_weight_in,
-    logits,
-    got,
-    items,
-    weights,
     bias,
     out_weight,
+    logits,
+    table,
+    early,
+    weights,
     tiles,
+    users,
     first,
+    state,
     rounded,
-    state,
     answer,
+    picks,
+    picked,
     sems,
 ):
-    pairs = [(got_in, got), (items_in, items), (bias_in, bias), (out_weight_in, out_weight)]
-    pairs += [(weights_in.at[i], weights.at[i]) for i in range(weights.shape[0])]
-    copies = [pltpu.make_async_copy(a, b, sems.at[i]) for i, (a, b) in enumerate(pairs)]
-    for copy in copies:
-        copy.start()
-    copies[0].wait()
     sources = got.shape[0]
     halves = 2
     per = chunk // halves
     rows = per * sources
-    width = state.shape[1]
-    layers = weights.shape[0]
-    features = items.shape[1]
-    d_user = width - features
+    layers, width, _ = weights_in.shape
+    chunks = width // LANES
+    double = 2 * chunks
+    d_user = 2 * LANES
+    pairs = [(weights_in.at[0, pl.ds(0, d_user)], early), (table_in, table)]
+    pairs += [(weights_in.at[i], weights.at[i - 1]) for i in range(1, layers)]
+    copies = [pltpu.make_async_copy(a, b, sems.at[i]) for i, (a, b) in enumerate(pairs)]
+    for copy in copies:
+        copy.start()
+    reqs = lax.axis_size("req")
     tiles[...] = got[...].astype(F32).reshape(sources * MSG, LANES)
     wanted = tiles[pl.ds(WANT_ROW, sources, stride=MSG), :]
-    people = jnp.concatenate(
-        [tiles[pl.ds(USER_ROW + i, sources, stride=MSG), :] for i in range(2)], axis=1
-    ).astype(BF16)
     lane = iota((sources, LANES), 1)
-    high_lane = (lane >= HALF) & (wanted > 0.0)
-    most = jnp.max(jnp.where(high_lane, lane - HALF + 1, 0))
-    reqs = lax.axis_size("req")
+    low = wanted.astype(I32)
+    high = pltpu.roll(wanted, HALF, axis=1).astype(I32)
+    within = low + 256 * (high & 3)
+    person = ((high >> 2) & 31) * reqs + iota((sources, LANES), 0) % reqs
+    split = (table.shape[0] - 1).bit_length()
+    picks[...] = within * double + ((person * double) << split)
+    copy = pltpu.make_async_copy(picks, picked, sems.at[len(copies)])
+    copy.start()
+    most = jnp.max(jnp.where((lane < HALF) & (high > 0), lane + 1, 0))
+    people = [tiles[pl.ds(USER_ROW + i, sources, stride=MSG), :] for i in range(2)]
+    flat = jnp.concatenate(people, axis=1).astype(BF16)
+    for c in range(chunks):
+        part = people[c] if c < 2 else jnp.zeros((sources, LANES), F32)
+        users[pl.ds(c, sources, stride=double), :] = part
+    copies[0].wait()
+    for c in range(0, chunks, 2):
+        to = slice(c * LANES, (c + 2) * LANES)
+        product = dot(flat, early[:, to]) + bias[0:1, to]
+        for i in range(2):
+            part = product[:, i * LANES : (i + 1) * LANES]
+            users[pl.ds(chunks + c + i, sources, stride=double), :] = part
     answer[...] = jnp.zeros(answer.shape, F32)
-    source = iota((rows, 1), 0) % sources
+    copy.wait()
+    copies[1].wait()
 
     def arrive(t, some):
         @pl.when(t == 0)
@@ -164,44 +217,50 @@
                 copy.wait()
 
     def step(t, carry):
-        arrive(t, copies[1:4])
+        def gather(s, carry):
+            values = []
+            for u in range(8):
+                source = s * 8 + u
+                for k in range(chunk):
+                    both = picked[source, t * chunk + k]
+                    row = pl.multiple_of(both & ((1 << split) - 1), double)
+                    man = pl.multiple_of(both >> split, double)
+                    start = table[pl.ds(row, chunks), :] + users[pl.ds(man, chunks), :]
+                    product = (
+                        table[pl.ds(row + chunks, chunks), :]
+                        + users[pl.ds(man + chunks, chunks), :]
+                    )
+                    values.append((k * sources + source, start, start * product + start))
+            for at, start, new in values:
+                first[pl.ds(at, chunks, stride=stretch), :] = start
+                state[pl.ds(at, chunks, stride=stretch), :] = new
+            return carry
+
+        lax.fori_loop(0, sources // 8, gather, 0)
         for h in range(halves):
             at = slice(h * rows, (h + 1) * rows)
-            lows, highs = [], []
-            for k in range(per):
-                j = t * chunk + h * per + k
-                lows.append(lane_sum(jnp.where(lane == j, wanted, 0.0)))
-                highs.append(lane_sum(jnp.where(lane == j + HALF, wanted, 0.0)))
-            low = jnp.concatenate(lows, axis=0).astype(I32)
-            high = jnp.concatenate(highs, axis=0).astype(I32)
-            within = low + 256 * (high & 3)
-            person = ((high >> 2) & 31) * reqs + source % reqs
-            pick_user = as_bf16(person == iota((rows, sources), 1))
-            pick_item = as_bf16(within == iota((rows, items.shape[0]), 1))
-            first[at, :d_user] = dot(pick_user, people).astype(BF16)
-            for n in range(0, features, block):
-                first[at, d_user + n : d_user + n + block] = dot(
-                    pick_item, items[:, n : n + block]
-                ).astype(BF16)
+            for c in range(chunks):
+                lines = slice(c * stretch + h * rows, c * stretch + (h + 1) * rows)
+                rounded[0, at, c * LANES : (c + 1) * LANES] = state[lines, :].astype(BF16)
         parts = [jnp.zeros((rows, LANES), F32) for _ in range(halves)]
-        for layer in range(layers):
-            if layer < 2:
-                arrive(t, copies[4:5] if layer == 0 else copies[5:])
+        for layer in range(1, layers):
+            if layer < 3:
+                arrive(t, copies[2:3] if layer == 1 else copies[3:])
             for h in range(halves):
                 at = slice(h * rows, (h + 1) * rows)
-                left = first[at, :] if layer == 0 else rounded[(layer + 1) % 2, at, :]
+                left = rounded[(layer + 1) % 2, at, :]
                 for n in range(0, width, block):
                     to = slice(n, n + block)
-                    product = dot(left, weights[layer, :, to]) + bias[layer : layer + 1, to]
-                    start = first[at, to].astype(F32)
-                    new = start * product + (start if layer == 0 else state[at, to])
-                    if layer < layers - 1:
-                        state[at, to] = new
-                        rounded[layer % 2, at, to] = new.astype(BF16)
-                    else:
-                        new = new * out_weight[:, to]
-                        for i in range(0, block, LANES):
-                            parts[h] = parts[h] + new[:, i : i + LANES]
+                    product = dot(left, weights[layer - 1, :, to]) + bias[layer : layer + 1, to]
+                    for i in range(0, block, LANES):
+                        c = (n + i) // LANES
+                        lines = slice(c * stretch + h * rows, c * stretch + (h + 1) * rows)
+                        new = first[lines, :] * product[:, i : i + LANES] + state[lines, :]
+                        if layer < layers - 1:
+                            state[lines, :] = new
+                            rounded[layer % 2, at, n + i : n + i + LANES] = new.astype(BF16)
+                        else:
+                            parts[h] = parts[h] + new * out_weight[:, n + i : n + i + LANES]
         for h in range(halves):
             value = lane_sum(parts[h])
             for k in range(per):
@@ -337,30 +396,50 @@
         user_emb,
     )
     got = lax.all_to_all(message, ("item", "req"), split_axis=0, concat_axis=0, tiled=True)
+    stored, features = item_features.shape
+    lines = stored * 2 * width // LANES
+    band = stored // 4
+    table = pl.pallas_call(
+        functools.partial(project_kernel, band),
+        out_shape=jax.ShapeDtypeStruct((lines, LANES), F32),
+        in_specs=[HBM, HBM],
+        out_specs=HBM,
+        scratch_shapes=[
+            pltpu.VMEM(item_features.shape, BF16),
+            pltpu.VMEM((features, width), BF16),
+            pltpu.VMEM((lines, LANES), F32),
+            pltpu.SemaphoreType.DMA((2 + stored // band,)),
+        ],
+        compiler_params=whole,
+        name="project",
+        cost_estimate=pl.CostEstimate(flops=2 << 30, bytes_accessed=12 << 20, transcendentals=0),
+    )(item_features, cross_weights)
     chunk = 4
     rows = chunk * owners
+    stretch = rows + 8
     answers = pl.pallas_call(
-        functools.partial(rank_kernel, chunk, 256),
+        functools.partial(rank_kernel, chunk, 256, stretch),
         out_shape=jax.ShapeDtypeStruct((owners, 1, LANES), F32),
-        in_specs=[HBM] * 5,
+        in_specs=[VMEM, HBM, HBM, VMEM, VMEM],
         out_specs=VMEM,
         scratch_shapes=[
-            pltpu.VMEM((owners, MSG, LANES), BF16),
-            pltpu.VMEM(item_features.shape, BF16),
-            pltpu.VMEM(cross_weights.shape, BF16),
-            pltpu.VMEM(cross_bias.shape, F32),
-            pltpu.VMEM((1, width), F32),
+            pltpu.VMEM((lines, LANES), F32),
+            pltpu.VMEM((d_user, width), BF16),
+            pltpu.VMEM((layers - 1, width, width), BF16),
             pltpu.VMEM((owners * MSG, LANES), F32),
-            pltpu.VMEM((rows, width), BF16),
+            pltpu.VMEM((owners * 2 * width // LANES, LANES), F32),
+            pltpu.VMEM((stretch * width // LANES, LANES), F32),
+            pltpu.VMEM((stretch * width // LANES, LANES), F32),
             pltpu.VMEM((2, rows, width), BF16),
-            pltpu.VMEM((rows, width), F32),
             pltpu.VMEM((owners, LANES), F32),
-            pltpu.SemaphoreType.DMA((4 + layers,)),
-        ],
-        compiler_params=whole,
+            pltpu.VMEM((owners, LANES), I32),
+            pltpu.SMEM((owners, LANES), I32),
+            pltpu.SemaphoreType.DMA((layers + 2,)),
+        ],
+        compiler_params=pltpu.CompilerParams(vmem_limit_bytes=52 << 20),
         name="rank",
         cost_estimate=pl.CostEstimate(flops=12 << 30, bytes_accessed=10 << 20, transcendentals=0),
-    )(got, item_features, cross_weights, cross_bias, out_weight.reshape(1, width))
+    )(got, table, cross_weights, cross_bias, out_weight.reshape(1, width))
     back = lax.all_to_all(answers, ("item", "req"), split_axis=0, concat_axis=0, tiled=True)
     looked = 14
     scores = pl.pallas_call(

time: 63 us -> 63.4 us (level)
  blocking collectives: 22.7 us -> 0 us
  starting transfers between devices: 9.21 us -> 21.5 us
  Pallas kernels: 29.4 us -> 37 us
  waiting for transfers between devices: 0.4 us -> 3.87 us
    all_to_all x1 -> x0, blocking collectives: 22.7 us -> none  [on_device(): lax.all_to_all(message, ('item', 'req'), split_axis=0, concat_axis=0, til...]
    all_to_all x0 -> x1, starting transfers between devices: none -> 11.5 us  [on_device(): lax.all_to_all(message, ('item', 'req'), split_axis=0, concat_axis=0, til...]
    pallas_call x1 -> x2, Pallas kernels: 15.7 us -> 23.3 us  [the longest x1 15.6 us: on_device(): pl.pallas_call(functools.partial(rank_kernel, chunk, 256, stretch), out_s...]
    all_to_all x0 -> x1, waiting for transfers between devices: none -> 3.42 us  [on_device(): lax.all_to_all(message, ('item', 'req'), split_axis=0, concat_axis=0, til...]
    all_to_all x1, starting transfers between devices: 9.21 us -> 9.95 us  [on_device(): lax.all_to_all(answers, ('item', 'req'), split_axis=0, concat_axis=0, til...]
  transfers between devices with their start and end apart: 1 -> 2, of which waited for: 1 -> 2; matrix products, arithmetic and copies ran while one was open for 0% -> 0% of each run, Pallas kernels for 15% -> 27%
where the time goes in v4:
time: 63.4 us; the launch traced here: 63 us
  Pallas kernels  37 us (58%)
  starting transfers between devices  21.5 us (34%)
  waiting for transfers between devices  3.87 us (6%)
  between operations  0.72 us (1%)
    pallas_call x1, Pallas kernels, on_device(): pl.pallas_call(functools.partial(rank_kernel, chunk, 256, stretch), out_s...  15.6 us
    all_to_all x1, starting transfers between devices, on_device(): lax.all_to_all(message, ('item', 'req'), split_axis=0, concat_axis=0, til...  11.5 us
    all_to_all x1, starting transfers between devices, on_device(): lax.all_to_all(answers, ('item', 'req'), split_axis=0, concat_axis=0, til...  9.95 us
    pallas_call x1, Pallas kernels, on_device(): pl.pallas_call(functools.partial(score_kernel, 512, looked), out_shape=ja...  9.14 us
    pallas_call x1, Pallas kernels, on_device(): pl.pallas_call(functools.partial(project_kernel, band), out_shape=jax.Sha...  7.67 us
    all_to_all x1, waiting for transfers between devices, on_device(): lax.all_to_all(message, ('item', 'req'), split_axis=0, concat_axis=0, til...  3.42 us
    pallas_call x1, Pallas kernels, on_device(): pl.pallas_call(prepare_kernel, out_shape=(jax.ShapeDtypeStruct((owners, M...  3.39 us
  transfers between devices with their start and end apart: 2, of which 2 were waited for; matrix products, arithmetic and copies ran while one was open for 0% of the time, Pallas kernels for 27%

profile of v4, /device:TPU:1, one launch (start us, length us, event | category | flops | bytes accessed | tf_op | source)
XLA Modules:
  0.0 63.0 jit_solution(12204621223682586404)
XLA Ops:
  0.6 3.4 %prepare.1 = (bf16[128,8,128]{2,1,0:T(8,128)(2,1)}, s32[512,128]{1,0:T(8,128)}) custom-call(s32[16,32]{1,0:T(8,128)} %bitcast.11, s32[1024,128]{1,0:T(8,128)} %bitcast.10, bf16[8,256]{1,0:T(8,128)(2,1)} %bitcast.13, bf16[32,256]{1,0:T(8,128)(2,1)} %user.1), custom_call_target="tpu_custom_call" | custom-call | tf_op jit(solution)/shard_map/prepare/pallas_call | solution.py:374
  4.0 11.5 %all-to-all-start = ((bf16[128,8,128]{2,1,0:T(8,128)(2,1)}), bf16[128,8,128]{2,1,0:T(8,128)(2,1)S(1)}, u32[]{:S(2)}, u32[]{:S(2)}) async-start(bf16[128,8,128]{2,1,0:T(8,128)(2,1)} %get-tuple-element.4), calls=%async_computation | async-start | bytes 524288 | tf_op jit(solution)/shard_map/all_to_all | solution.py:398
  15.5 0.0 copy-start.3
  15.6 0.0 copy-start.4
  15.6 7.7 %project.1.table_in = f32[16384,128]{1,0:T(8,128)} custom-call(bf16[1024,768]{1,0:T(8,128)(2,1)} %items_in.1, bf16[4,1024,1024]{2,1,0:T(8,128)(2,1)} %weights_in.3), custom_call_target="tpu_custom_call" | custom-call | flops 2147483648 | bytes 12582912 | tf_op jit(solution)/shard_map/project/pallas_call | solution.py:402
  23.2 3.4 %all-to-all-done.got = bf16[128,8,128]{2,1,0:T(8,128)(2,1)S(1)} async-done(((bf16[128,8,128]{2,1,0:T(8,128)(2,1)}), bf16[128,8,128]{2,1,0:T(8,128)(2,1)S(1)}, u32[]{:S(2)}, u32[]{:S(2)}) %all-to-all-start) | async-done | bytes 262176 | tf_op jit(solution)/shard_map/all_to_all | solution.py:398
  26.7 0.0 copy-done.3
  26.7 0.0 copy-done.4
  26.7 0.0 copy-start.1
  26.7 0.0 copy-start.2
  26.7 0.0 copy-start
  26.7 15.6 %rank.1 = f32[128,1,128]{2,1,0:T(1,128)} custom-call(bf16[128,8,128]{2,1,0:T(8,128)(2,1)S(1)} %all-to-all-done.got, f32[16384,128]{1,0:T(8,128)} %project.1.table_in, bf16[4,1024,1024]{2,1,0:T(8,128)(2,1)} %weights_in.3, f32[4,1024]{1,0:T(4,128)S(1)} %copy-done.3, f32[1,1024]{1,0:T(1,128)S(1)} %bitcast.9), custom_call_target="tpu_custom_call" | custom-call | flops 12884901888 | bytes 10485760 | tf_op jit(solution)/shard_map/rank/pallas_call | solution.py:420
  42.3 10.0 %all-to-all-start.1 = ((f32[128,1,128]{2,1,0:T(1,128)}), f32[128,1,128]{2,1,0:T(1,128)S(1)}, u32[]{:S(2)}, u32[]{:S(2)}) async-start(f32[128,1,128]{2,1,0:T(1,128)} %rank.1), calls=%async_computation.1 | async-start | bytes 131072 | tf_op jit(solution)/shard_map/all_to_all | solution.py:443
  52.3 0.0 copy-done.1
  52.3 0.0 copy-done.2
  52.3 9.1 %scores.1 = f32[32,4096]{1,0:T(8,128)} custom-call(bf16[128,8,128]{2,1,0:T(8,128)(2,1)S(1)} %all-to-all-done.got, bf16[32,256]{1,0:T(8,128)(2,1)S(1)} %copy-done.1, s32[32,4096]{1,0:T(8,128)S(1)} %bitcast.8), custom_call_target="tpu_custom_call" | custom-call | flops 2147483648 | bytes 41943040 | tf_op jit(solution)/shard_map/scores/pallas_call | solution.py:445
  61.4 0.4 all-to-all-done.1.back
  61.9 0.0 copy-done
  61.9 1.2 %collect.1 = f32[16,32]{1,0:T(8,128)} custom-call(f32[128,1,128]{2,1,0:T(1,128)S(1)} %all-to-all-done.1.back, s32[512,128]{1,0:T(8,128)S(1)} %copy-done), custom_call_target="tpu_custom_call" | custom-call | tf_op jit(solution)/shard_map/collect/pallas_call | solution.py:459
Async XLA Ops:
  4.0 22.6 %all-to-all-start = ((bf16[128,8,128]{2,1,0:T(8,128)(2,1)}), bf16[128,8,128]{2,1,0:T(8,128)(2,1)S(1)}, u32[]{:S(2)}, u32[]{:S(2)}) async-start(bf16[128,8,128]{2,1,0:T(8,128)(2,1)} %get-tuple-element.4), calls=%async_computation | async-start | bytes 524288 | tf_op jit(solution)/shard_map/all_to_all | solution.py:398
  15.5 11.1 %copy-start.3 = (f32[4,1024]{1,0:T(4,128)S(1)}, f32[4,1024]{1,0:T(4,128)}, u32[]{:S(2)}) copy-start(f32[4,1024]{1,0:T(4,128)} %bias.1) | copy-start | bytes 49156
  15.6 11.1 %copy-start.4 = (f32[1024]{0:T(1024)S(1)}, f32[1024]{0:T(1024)}, u32[]{:S(2)}) copy-start(f32[1024]{0:T(1024)} %param.17) | copy-start | bytes 12292
  26.7 25.6 %copy-start.1 = (bf16[32,256]{1,0:T(8,128)(2,1)S(1)}, bf16[32,256]{1,0:T(8,128)(2,1)}, u32[]{:S(2)}) copy-start(bf16[32,256]{1,0:T(8,128)(2,1)} %user.1) | copy-start | bytes 49156
  26.7 25.6 %copy-start.2 = (s32[4096,32]{0,1:T(8,128)S(1)}, s32[4096,32]{0,1:T(8,128)}, u32[]{:S(2)}) copy-start(s32[4096,32]{0,1:T(8,128)} %param.11) | copy-start | bytes 1572868
  26.7 35.2 %copy-start = (s32[512,128]{1,0:T(8,128)S(1)}, s32[512,128]{1,0:T(8,128)}, u32[]{:S(2)}) copy-start(s32[512,128]{1,0:T(8,128)} %get-tuple-element.5.meta) | copy-start | bytes 786436
  42.3 19.6 %all-to-all-start.1 = ((f32[128,1,128]{2,1,0:T(1,128)}), f32[128,1,128]{2,1,0:T(1,128)S(1)}, u32[]{:S(2)}, u32[]{:S(2)}) async-start(f32[128,1,128]{2,1,0:T(1,128)} %rank.1), calls=%async_computation.1 | async-start | bytes 131072 | tf_op jit(solution)/shard_map/all_to_all | solution.py:443

commit v5 on v4

--- a/solution.py
+++ b/solution.py
@@ -113,32 +113,24 @@
 def project_kernel(band, items_in, weights_in, table, items, weights, tiles, sems):
     stored, features = items.shape
     width = weights.shape[1]
-    d_user = width - features
     copies = [
         pltpu.make_async_copy(items_in, items, sems.at[0]),
-        pltpu.make_async_copy(weights_in.at[0, pl.ds(d_user, features)], weights, sems.at[1]),
+        pltpu.make_async_copy(weights_in.at[0, pl.ds(width - features, features)], weights, sems.at[1]),
     ]
     for copy in copies:
         copy.start()
     for copy in copies:
         copy.wait()
     chunks = width // LANES
-    lines = band * 2 * chunks
     copies = []
     for n in range(stored // band):
-        rows = slice(n * band, (n + 1) * band)
-        for c in range(chunks):
-            at = c * LANES - d_user
-            part = jnp.zeros((band, LANES), F32)
-            if at >= 0:
-                part = items[rows, at : at + LANES].astype(F32)
-            tiles[pl.ds(n * lines + c, band, stride=2 * chunks), :] = part
         for c in range(0, chunks, 2):
-            product = dot(items[rows, :], weights[:, c * LANES : (c + 2) * LANES])
+            left = items[n * band : (n + 1) * band, :]
+            product = dot(left, weights[:, c * LANES : (c + 2) * LANES])
             for i in range(2):
-                to = pl.ds(n * lines + chunks + c + i, band, stride=2 * chunks)
+                to = pl.ds(n * band * chunks + c + i, band, stride=chunks)
                 tiles[to, :] = product[:, i * LANES : (i + 1) * LANES]
-        whole = pl.ds(n * lines, lines)
+        whole = pl.ds(n * band * chunks, band * chunks)
         copies.append(pltpu.make_async_copy(tiles.at[whole], table.at[whole], sems.at[2 + n]))
         copies[-1].start()
     for copy in copies:
@@ -146,20 +138,24 @@
 
 
 def rank_kernel(
-    chunk,
+    ranks,
     block,
     stretch,
     got,
     table_in,
+    items_in,
     weights_in,
     bias,
     out_weight,
     logits,
     table,
+    items,
     early,
     weights,
     tiles,
-    users,
+    features,
+    people,
+    greetings,
     first,
     state,
     rounded,
@@ -169,16 +165,18 @@
     sems,
 ):
     sources = got.shape[0]
-    halves = 2
-    per = chunk // halves
-    rows = per * sources
+    rows = ranks * sources
     layers, width, _ = weights_in.shape
+    stored = items.shape[0]
     chunks = width // LANES
-    double = 2 * chunks
-    d_user = 2 * LANES
-    pairs = [(weights_in.at[0, pl.ds(0, d_user)], early), (table_in, table)]
-    pairs += [(weights_in.at[i], weights.at[i - 1]) for i in range(1, layers)]
-    copies = [pltpu.make_async_copy(a, b, sems.at[i]) for i, (a, b) in enumerate(pairs)]
+    own = early.shape[0] // LANES
+    copies = [
+        (weights_in.at[0, pl.ds(0, own * LANES)], early),
+        (items_in, items),
+        (table_in, table),
+    ]
+    copies += [(weights_in.at[i], weights.at[i - 1]) for i in range(1, layers)]
+    copies = [pltpu.make_async_copy(a, b, sems.at[i]) for i, (a, b) in enumerate(copies)]
     for copy in copies:
         copy.start()
     reqs = lax.axis_size("req")
@@ -189,87 +187,109 @@
     high = pltpu.roll(wanted, HALF, axis=1).astype(I32)
     within = low + 256 * (high & 3)
     person = ((high >> 2) & 31) * reqs + iota((sources, LANES), 0) % reqs
-    split = (table.shape[0] - 1).bit_length()
-    picks[...] = within * double + ((person * double) << split)
-    copy = pltpu.make_async_copy(picks, picked, sems.at[len(copies)])
-    copy.start()
+    split = (stored * chunks - 1).bit_length()
+    picks[...] = within * chunks + ((person * chunks) << split)
+    fetch = pltpu.make_async_copy(picks, picked, sems.at[len(copies)])
+    fetch.start()
     most = jnp.max(jnp.where((lane < HALF) & (high > 0), lane + 1, 0))
-    people = [tiles[pl.ds(USER_ROW + i, sources, stride=MSG), :] for i in range(2)]
-    flat = jnp.concatenate(people, axis=1).astype(BF16)
+    users = [tiles[pl.ds(USER_ROW + i, sources, stride=MSG), :] for i in range(own)]
+    blank = jnp.zeros((sources, LANES), F32)
     for c in range(chunks):
-        part = people[c] if c < 2 else jnp.zeros((sources, LANES), F32)
-        users[pl.ds(c, sources, stride=double), :] = part
+        people[pl.ds(c, sources, stride=chunks), :] = users[c] if c < own else blank
     copies[0].wait()
+    flat = jnp.concatenate(users, axis=1).astype(BF16)
     for c in range(0, chunks, 2):
         to = slice(c * LANES, (c + 2) * LANES)
         product = dot(flat, early[:, to]) + bias[0:1, to]
         for i in range(2):
             part = product[:, i * LANES : (i + 1) * LANES]
-            users[pl.ds(chunks + c + i, sources, stride=double), :] = part
+            greetings[pl.ds(c + i, sources, stride=chunks), :] = part
+    copies[1].wait()
+    for c in range(chunks):
+        part = jnp.zeros((stored, LANES), F32)
+        if c >= own:
+            part = items[:, (c - own) * LANES : (c - own + 1) * LANES].astype(F32)
+        features[pl.ds(c, stored, stride=chunks), :] = part
     answer[...] = jnp.zeros(answer.shape, F32)
-    copy.wait()
-    copies[1].wait()
-
-    def arrive(t, some):
-        @pl.when(t == 0)
-        def _():
-            for copy in some:
-                copy.wait()
-
-    def step(t, carry):
-        def gather(s, carry):
+    fetch.wait()
+    copies[2].wait()
+
+    def gather(slot, unit, some):
+        values = []
+        for n in some:
+            k, source = n // sources, n % sources
+            both = picked[source, unit * ranks + k]
+            row = pl.ds(pl.multiple_of(both & ((1 << split) - 1), chunks), chunks)
+            man = pl.ds(pl.multiple_of(both >> split, chunks), chunks)
+            start = features[row, :] + people[man, :]
+            values.append((n, start, start * (table[row, :] + greetings[man, :]) + start))
+        for n, start, new in values:
+            first[slot, pl.ds(n, chunks, stride=stretch), :] = start
+            state[slot, pl.ds(n, chunks, stride=stretch), :] = new
+
+    def lines(c):
+        return slice(c * stretch, c * stretch + rows)
+
+    def run(slot, unit, waits):
+        following = list(range(rows))
+        parts = jnp.zeros((rows, LANES), F32)
+        left = layers - 1
+        share = -(-rows // (left * width // block))
+        for c in range(chunks):
+            rounded[0, :, c * LANES : (c + 1) * LANES] = state[slot, lines(c), :].astype(BF16)
+        for layer in range(1, layers):
+            if waits is not None and layer < 3:
+                waits(copies[3:4] if layer == 1 else copies[4:])
+            source = rounded[(layer + 1) % 2]
+            for n in range(0, width, block):
+                product = dot(source, weights[layer - 1, :, n : n + block])
+                product = product + bias[layer : layer + 1, n : n + block]
+                gather(1 - slot, unit + 1, following[:share])
+                following = following[share:]
+                for i in range(0, block, LANES):
+                    at = lines((n + i) // LANES)
+                    new = first[slot, at, :] * product[:, i : i + LANES] + state[slot, at, :]
+                    if layer < layers - 1:
+                        state[slot, at, :] = new
+                        rounded[layer % 2, :, n + i : n + i + LANES] = new.astype(BF16)
+                    else:
+                        parts = parts + new * out_weight[:, n + i : n + i + LANES]
+        value = lane_sum(parts)
+        for k in range(ranks):
+            mine = value[k * sources : (k + 1) * sources]
+            answer[...] += jnp.where(lane == unit * ranks + k, mine, 0.0)
+
+    def begin(s, carry):
+        for k in range(ranks):
             values = []
             for u in range(8):
                 source = s * 8 + u
-                for k in range(chunk):
-                    both = picked[source, t * chunk + k]
-                    row = pl.multiple_of(both & ((1 << split) - 1), double)
-                    man = pl.multiple_of(both >> split, double)
-                    start = table[pl.ds(row, chunks), :] + users[pl.ds(man, chunks), :]
-                    product = (
-                        table[pl.ds(row + chunks, chunks), :]
-                        + users[pl.ds(man + chunks, chunks), :]
-                    )
-                    values.append((k * sources + source, start, start * product + start))
-            for at, start, new in values:
-                first[pl.ds(at, chunks, stride=stretch), :] = start
-                state[pl.ds(at, chunks, stride=stretch), :] = new
-            return carry
-
-        lax.fori_loop(0, sources // 8, gather, 0)
-        for h in range(halves):
-            at = slice(h * rows, (h + 1) * rows)
-            for c in range(chunks):
-                lines = slice(c * stretch + h * rows, c * stretch + (h + 1) * rows)
-                rounded[0, at, c * LANES : (c + 1) * LANES] = state[lines, :].astype(BF16)
-        parts = [jnp.zeros((rows, LANES), F32) for _ in range(halves)]
-        for layer in range(1, layers):
-            if layer < 3:
-                arrive(t, copies[2:3] if layer == 1 else copies[3:])
-            for h in range(halves):
-                at = slice(h * rows, (h + 1) * rows)
-                left = rounded[(layer + 1) % 2, at, :]
-                for n in range(0, width, block):
-                    to = slice(n, n + block)
-                    product = dot(left, weights[layer - 1, :, to]) + bias[layer : layer + 1, to]
-                    for i in range(0, block, LANES):
-                        c = (n + i) // LANES
-                        lines = slice(c * stretch + h * rows, c * stretch + (h + 1) * rows)
-                        new = first[lines, :] * product[:, i : i + LANES] + state[lines, :]
-                        if layer < layers - 1:
-                            state[lines, :] = new
-                            rounded[layer % 2, at, n + i : n + i + LANES] = new.astype(BF16)
-                        else:
-                            parts[h] = parts[h] + new * out_weight[:, n + i : n + i + LANES]
-        for h in range(halves):
-            value = lane_sum(parts[h])
-            for k in range(per):
-                j = t * chunk + h * per + k
-                mine = value[k * sources : (k + 1) * sources]
-                answer[...] += jnp.where(lane == j, mine, 0.0)
+                both = picked[source, k]
+                row = pl.ds(pl.multiple_of(both & ((1 << split) - 1), chunks), chunks)
+                man = pl.ds(pl.multiple_of(both >> split, chunks), chunks)
+                start = features[row, :] + people[man, :]
+                new = start * (table[row, :] + greetings[man, :]) + start
+                values.append((k * sources + source, start, new))
+            for n, start, new in values:
+                first[0, pl.ds(n, chunks, stride=stretch), :] = start
+                state[0, pl.ds(n, chunks, stride=stretch), :] = new
         return carry
 
-    lax.fori_loop(0, jnp.maximum((most + chunk - 1) // chunk, 1), step, 0)
+    lax.fori_loop(0, sources // 8, begin, 0)
+
+    def step(t, carry):
+        def waits(some):
+            @pl.when(t == 0)
+            def _():
+                for copy in some:
+                    copy.wait()
+
+        run(0, 2 * t, waits)
+        run(1, 2 * t + 1, None)
+        return carry
+
+    steps = jnp.maximum((most + 2 * ranks - 1) // (2 * ranks), 1)
+    lax.fori_loop(0, steps, step, 0)
     logits[...] = answer[...].reshape(logits.shape)
 
 
@@ -397,7 +417,8 @@
     )
     got = lax.all_to_all(message, ("item", "req"), split_axis=0, concat_axis=0, tiled=True)
     stored, features = item_features.shape
-    lines = stored * 2 * width // LANES
+    chunks = width // LANES
+    lines = stored * chunks
     band = stored // 4
     table = pl.pallas_call(
         functools.partial(project_kernel, band),
@@ -414,32 +435,35 @@
         name="project",
         cost_estimate=pl.CostEstimate(flops=2 << 30, bytes_accessed=12 << 20, transcendentals=0),
     )(item_features, cross_weights)
-    chunk = 4
-    rows = chunk * owners
+    ranks = 2
+    rows = ranks * owners
     stretch = rows + 8
     answers = pl.pallas_call(
-        functools.partial(rank_kernel, chunk, 256, stretch),
+        functools.partial(rank_kernel, ranks, 256, stretch),
         out_shape=jax.ShapeDtypeStruct((owners, 1, LANES), F32),
-        in_specs=[VMEM, HBM, HBM, VMEM, VMEM],
+        in_specs=[VMEM, HBM, HBM, HBM, VMEM, VMEM],
         out_specs=VMEM,
         scratch_shapes=[
             pltpu.VMEM((lines, LANES), F32),
+            pltpu.VMEM(item_features.shape, BF16),
             pltpu.VMEM((d_user, width), BF16),
             pltpu.VMEM((layers - 1, width, width), BF16),
             pltpu.VMEM((owners * MSG, LANES), F32),
-            pltpu.VMEM((owners * 2 * width // LANES, LANES), F32),
-            pltpu.VMEM((stretch * width // LANES, LANES), F32),
-            pltpu.VMEM((stretch * width // LANES, LANES), F32),
+            pltpu.VMEM((lines, LANES), F32),
+            pltpu.VMEM((owners * chunks, LANES), F32),
+            pltpu.VMEM((owners * chunks, LANES), F32),
+            pltpu.VMEM((2, stretch * chunks, LANES), F32),
+            pltpu.VMEM((2, stretch * chunks, LANES), F32),
             pltpu.VMEM((2, rows, width), BF16),
             pltpu.VMEM((owners, LANES), F32),
             pltpu.VMEM((owners, LANES), I32),
             pltpu.SMEM((owners, LANES), I32),
-            pltpu.SemaphoreType.DMA((layers + 2,)),
+            pltpu.SemaphoreType.DMA((layers + 3,)),
         ],
-        compiler_params=pltpu.CompilerParams(vmem_limit_bytes=52 << 20),
+        compiler_params=pltpu.CompilerParams(vmem_limit_bytes=53 << 20),
         name="rank",
         cost_estimate=pl.CostEstimate(flops=12 << 30, bytes_accessed=10 << 20, transcendentals=0),
-    )(got, table, cross_weights, cross_bias, out_weight.reshape(1, width))
+    )(got, table, item_features, cross_weights, cross_bias, out_weight.reshape(1, width))
     back = lax.all_to_all(answers, ("item", "req"), split_axis=0, concat_axis=0, tiled=True)
     looked = 14
     scores = pl.pallas_call(

time: 63.4 us -> 61.1 us (0.964)
  Pallas kernels: 37 us -> 33.7 us
  waiting for transfers between devices: 3.87 us -> 6.52 us
  starting transfers between devices: 21.5 us -> 19.7 us
    all_to_all x1, waiting for transfers between devices: 3.42 us -> 6.14 us  [on_device(): lax.all_to_all(message, ('item', 'req'), split_axis=0, concat_axis=0, til...]
    pallas_call x1, Pallas kernels: 7.67 us -> 4.96 us  [on_device(): pl.pallas_call(functools.partial(project_kernel, band), out_shape=jax.Sha...]
    all_to_all x1, starting transfers between devices: 9.95 us -> 8.2 us  [on_device(): lax.all_to_all(answers, ('item', 'req'), split_axis=0, concat_axis=0, til...]
  transfers between devices with their start and end apart: 2 -> 2, of which waited for: 2 -> 2; matrix products, arithmetic and copies ran while one was open for 0% -> 0% of each run, Pallas kernels for 27% -> 23%
where the time goes in v5:
time: 61.1 us; the launch traced here: 60.7 us
  Pallas kernels  33.7 us (55%)
  starting transfers between devices  19.7 us (32%)
  waiting for transfers between devices  6.52 us (11%)
  between operations  0.72 us (1%)
    pallas_call x1, Pallas kernels, on_device(): pl.pallas_call(functools.partial(rank_kernel, ranks, 256, stretch), out_s...  15.1 us
    all_to_all x1, starting transfers between devices, on_device(): lax.all_to_all(message, ('item', 'req'), split_axis=0, concat_axis=0, til...  11.5 us
    pallas_call x1, Pallas kernels, on_device(): pl.pallas_call(functools.partial(score_kernel, 512, looked), out_shape=ja...  9.14 us
    all_to_all x1, starting transfers between devices, on_device(): lax.all_to_all(answers, ('item', 'req'), split_axis=0, concat_axis=0, til...  8.2 us
    all_to_all x1, waiting for transfers between devices, on_device(): lax.all_to_all(message, ('item', 'req'), split_axis=0, concat_axis=0, til...  6.14 us
    pallas_call x1, Pallas kernels, on_device(): pl.pallas_call(functools.partial(project_kernel, band), out_shape=jax.Sha...  4.96 us
    pallas_call x1, Pallas kernels, on_device(): pl.pallas_call(prepare_kernel, out_shape=(jax.ShapeDtypeStruct((owners, M...  3.39 us
  transfers between devices with their start and end apart: 2, of which 2 were waited for; matrix products, arithmetic and copies ran while one was open for 0% of the time, Pallas kernels for 23%

profile of v5, /device:TPU:1, one launch (start us, length us, event | category | flops | bytes accessed | tf_op | source)
XLA Modules:
  0.0 60.7 jit_solution(17255630696219217777)
XLA Ops:
  0.6 3.4 %prepare.1 = (bf16[128,8,128]{2,1,0:T(8,128)(2,1)}, s32[512,128]{1,0:T(8,128)}) custom-call(s32[16,32]{1,0:T(8,128)} %bitcast.11, s32[1024,128]{1,0:T(8,128)} %bitcast.10, bf16[8,256]{1,0:T(8,128)(2,1)} %bitcast.13, bf16[32,256]{1,0:T(8,128)(2,1)} %user.1), custom_call_target="tpu_custom_call" | custom-call | tf_op jit(solution)/shard_map/prepare/pallas_call | solution.py:394
  4.0 11.5 %all-to-all-start = ((bf16[128,8,128]{2,1,0:T(8,128)(2,1)}), bf16[128,8,128]{2,1,0:T(8,128)(2,1)S(1)}, u32[]{:S(2)}, u32[]{:S(2)}) async-start(bf16[128,8,128]{2,1,0:T(8,128)(2,1)} %get-tuple-element.4), calls=%async_computation | async-start | bytes 524288 | tf_op jit(solution)/shard_map/all_to_all | solution.py:418
  15.5 0.0 copy-start.3
  15.6 0.0 copy-start.4
  15.6 5.0 %project.1.table_in = f32[8192,128]{1,0:T(8,128)} custom-call(bf16[1024,768]{1,0:T(8,128)(2,1)} %items_in.3, bf16[4,1024,1024]{2,1,0:T(8,128)(2,1)} %weights_in.3), custom_call_target="tpu_custom_call" | custom-call | flops 2147483648 | bytes 12582912 | tf_op jit(solution)/shard_map/project/pallas_call | solution.py:423
  20.5 6.1 %all-to-all-done.got = bf16[128,8,128]{2,1,0:T(8,128)(2,1)S(1)} async-done(((bf16[128,8,128]{2,1,0:T(8,128)(2,1)}), bf16[128,8,128]{2,1,0:T(8,128)(2,1)S(1)}, u32[]{:S(2)}, u32[]{:S(2)}) %all-to-all-start) | async-done | bytes 262176 | tf_op jit(solution)/shard_map/all_to_all | solution.py:418
  26.7 0.0 copy-done.3
  26.7 0.0 copy-done.4
  26.7 0.0 copy-start.1
  26.7 0.0 copy-start.2
  26.7 15.1 %rank.1 = f32[128,1,128]{2,1,0:T(1,128)} custom-call(bf16[128,8,128]{2,1,0:T(8,128)(2,1)S(1)} %all-to-all-done.got, f32[8192,128]{1,0:T(8,128)} %project.1.table_in, bf16[1024,768]{1,0:T(8,128)(2,1)} %items_in.3, bf16[4,1024,1024]{2,1,0:T(8,128)(2,1)} %weights_in.3, f32[4,1024]{1,0:T(4,128)S(1)} %copy-done.3, f32[1,1024]{1,0:T(1,128)S(1)} %bitcast.9), custom_call_target="tpu_custom_call" | custom-call | flops 12884901888 | bytes 10485760 | tf_op jit(solution)/shard_map/rank/pallas_call | solution.py:441
  41.8 0.0 copy-start
  41.8 8.2 %all-to-all-start.1 = ((f32[128,1,128]{2,1,0:T(1,128)}), f32[128,1,128]{2,1,0:T(1,128)S(1)}, u32[]{:S(2)}, u32[]{:S(2)}) async-start(f32[128,1,128]{2,1,0:T(1,128)} %rank.1), calls=%async_computation.1 | async-start | bytes 131072 | tf_op jit(solution)/shard_map/all_to_all | solution.py:467
  50.0 0.0 copy-done.1
  50.0 0.0 copy-done.2
  50.0 9.1 %scores.1 = f32[32,4096]{1,0:T(8,128)} custom-call(bf16[128,8,128]{2,1,0:T(8,128)(2,1)S(1)} %all-to-all-done.got, bf16[32,256]{1,0:T(8,128)(2,1)S(1)} %copy-done.1, s32[32,4096]{1,0:T(8,128)S(1)} %bitcast.8), custom_call_target="tpu_custom_call" | custom-call | flops 2147483648 | bytes 41943040 | tf_op jit(solution)/shard_map/scores/pallas_call | solution.py:469
  59.1 0.4 all-to-all-done.1.back
  59.5 0.0 copy-done
  59.5 1.2 %collect.1 = f32[16,32]{1,0:T(8,128)} custom-call(f32[128,1,128]{2,1,0:T(1,128)S(1)} %all-to-all-done.1.back, s32[512,128]{1,0:T(8,128)S(1)} %copy-done), custom_call_target="tpu_custom_call" | custom-call | tf_op jit(solution)/shard_map/collect/pallas_call | solution.py:483
Async XLA Ops:
  4.0 22.6 %all-to-all-start = ((bf16[128,8,128]{2,1,0:T(8,128)(2,1)}), bf16[128,8,128]{2,1,0:T(8,128)(2,1)S(1)}, u32[]{:S(2)}, u32[]{:S(2)}) async-start(bf16[128,8,128]{2,1,0:T(8,128)(2,1)} %get-tuple-element.4), calls=%async_computation | async-start | bytes 524288 | tf_op jit(solution)/shard_map/all_to_all | solution.py:418
  15.5 11.1 %copy-start.3 = (f32[4,1024]{1,0:T(4,128)S(1)}, f32[4,1024]{1,0:T(4,128)}, u32[]{:S(2)}) copy-start(f32[4,1024]{1,0:T(4,128)} %bias.1) | copy-start | bytes 49156
  15.6 11.1 %copy-start.4 = (f32[1024]{0:T(1024)S(1)}, f32[1024]{0:T(1024)}, u32[]{:S(2)}) copy-start(f32[1024]{0:T(1024)} %param.17) | copy-start | bytes 12292
  26.7 23.3 %copy-start.1 = (bf16[32,256]{1,0:T(8,128)(2,1)S(1)}, bf16[32,256]{1,0:T(8,128)(2,1)}, u32[]{:S(2)}) copy-start(bf16[32,256]{1,0:T(8,128)(2,1)} %user.1) | copy-start | bytes 49156
  26.7 23.3 %copy-start.2 = (s32[4096,32]{0,1:T(8,128)S(1)}, s32[4096,32]{0,1:T(8,128)}, u32[]{:S(2)}) copy-start(s32[4096,32]{0,1:T(8,128)} %param.11) | copy-start | bytes 1572868
  41.8 17.8 %copy-start = (s32[512,128]{1,0:T(8,128)S(1)}, s32[512,128]{1,0:T(8,128)}, u32[]{:S(2)}) copy-start(s32[512,128]{1,0:T(8,128)} %get-tuple-element.5.meta) | copy-start | bytes 786436
  41.8 17.7 %all-to-all-start.1 = ((f32[128,1,128]{2,1,0:T(1,128)}), f32[128,1,128]{2,1,0:T(1,128)S(1)}, u32[]{:S(2)}, u32[]{:S(2)}) async-start(f32[128,1,128]{2,1,0:T(1,128)} %rank.1), calls=%async_computation.1 | async-start | bytes 131072 | tf_op jit(solution)/shard_map/all_to_all | solution.py:467

commit v6 on v5

--- a/solution.py
+++ b/solution.py
@@ -44,14 +44,34 @@
     copies = [pltpu.make_async_copy(a, b, sems.at[i]) for i, (a, b) in enumerate(pairs)]
     for copy in copies:
         copy.start()
-    for copy in copies:
-        copy.wait()
     cand_dev, requests = cand.shape
     total = cand_dev * requests
     owners = message.shape[0]
     blocks = place.shape[0]
     item = lax.axis_index("item")
     req = lax.axis_index("req")
+    copies[2].wait()
+    copies[3].wait()
+    book = codebook[...].astype(F32)
+    sub = iota(book.shape, 0)
+    first = jnp.sum(jnp.where(sub == 2 * req, book, 0.0), axis=0, keepdims=True)
+    second = jnp.sum(jnp.where(sub == 2 * req + 1, book, 0.0), axis=0, keepdims=True)
+    people = user[...].astype(F32)
+    person = jnp.sum(jnp.where(iota(people.shape, 0) == item, people, 0.0), axis=0, keepdims=True)
+    tile = jnp.concatenate(
+        [
+            first[:, :LANES],
+            first[:, LANES:],
+            second[:, :LANES],
+            second[:, LANES:],
+            person[:, :LANES],
+            person[:, LANES:],
+            jnp.zeros((2, LANES), F32),
+        ],
+        axis=0,
+    )
+    tiles[...] = jnp.broadcast_to(tile[None], (owners, MSG, LANES)).reshape(owners * MSG, LANES)
+    copies[0].wait()
     ids = cand[...].astype(F32)
     spread = jnp.concatenate(
         [jnp.broadcast_to(ids[c : c + 1, :], (requests, requests)) for c in range(cand_dev)], axis=0
@@ -60,6 +80,7 @@
     diagonal = own_request == iota((total, requests), 1)
     ids = lane_sum(jnp.where(diagonal, spread, 0.0)).astype(I32)
     where_row = as_bf16((ids >> 7) == iota((total, blocks), 1))
+    copies[1].wait()
     stored = place[...]
     parts = jnp.concatenate(
         [
@@ -87,25 +108,6 @@
     high = ((within >> 8) + 4 * request + 128).astype(F32)
     entry = jnp.where(lane == rank, low, 0.0) + jnp.where(lane == rank + HALF, high, 0.0)
     wanted = dot(hits, entry.astype(BF16), (((0,), (0,)), ((), ())))
-    book = codebook[...].astype(F32)
-    sub = iota(book.shape, 0)
-    first = jnp.sum(jnp.where(sub == 2 * req, book, 0.0), axis=0, keepdims=True)
-    second = jnp.sum(jnp.where(sub == 2 * req + 1, book, 0.0), axis=0, keepdims=True)
-    people = user[...].astype(F32)
-    person = jnp.sum(jnp.where(iota(people.shape, 0) == item, people, 0.0), axis=0, keepdims=True)
-    tile = jnp.concatenate(
-        [
-            first[:, :LANES],
-            first[:, LANES:],
-            second[:, :LANES],
-            second[:, LANES:],
-            person[:, :LANES],
-            person[:, LANES:],
-            jnp.zeros((2, LANES), F32),
-        ],
-        axis=0,
-    )
-    tiles[...] = jnp.broadcast_to(tile[None], (owners, MSG, LANES)).reshape(owners * MSG, LANES)
     tiles[pl.ds(WANT_ROW, owners, stride=MSG), :] = wanted
     message[...] = tiles[...].reshape(owners, MSG, LANES).astype(BF16)
 
@@ -138,6 +140,7 @@
 
 
 def rank_kernel(
+    units,
     ranks,
     block,
     stretch,
@@ -191,19 +194,25 @@
     picks[...] = within * chunks + ((person * chunks) << split)
     fetch = pltpu.make_async_copy(picks, picked, sems.at[len(copies)])
     fetch.start()
-    most = jnp.max(jnp.where((lane < HALF) & (high > 0), lane + 1, 0))
     users = [tiles[pl.ds(USER_ROW + i, sources, stride=MSG), :] for i in range(own)]
     blank = jnp.zeros((sources, LANES), F32)
     for c in range(chunks):
         people[pl.ds(c, sources, stride=chunks), :] = users[c] if c < own else blank
     copies[0].wait()
     flat = jnp.concatenate(users, axis=1).astype(BF16)
-    for c in range(0, chunks, 2):
-        to = slice(c * LANES, (c + 2) * LANES)
-        product = dot(flat, early[:, to]) + bias[0:1, to]
-        for i in range(2):
-            part = product[:, i * LANES : (i + 1) * LANES]
-            greetings[pl.ds(c + i, sources, stride=chunks), :] = part
+    def greet(sums):
+        left = jnp.concatenate([flat] * (ranks // 2), axis=0)
+        for turn in range(width // block):
+            to = slice(turn * block, (turn + 1) * block)
+            pltpu.matmul_push_rhs(early[:, to], turn // 2, turn % 2)
+            pltpu.matmul_acc_lhs(sums[turn], left, turn // 2)
+        for turn in range(width // block):
+            product = pltpu.matmul_pop(sums[turn])[:sources]
+            product = product + bias[0:1, turn * block : (turn + 1) * block]
+            for i in range(0, block, LANES):
+                c = (turn * block + i) // LANES
+                greetings[pl.ds(c, sources, stride=chunks), :] = product[:, i : i + LANES]
+
     copies[1].wait()
     for c in range(chunks):
         part = jnp.zeros((stored, LANES), F32)
@@ -227,37 +236,8 @@
             first[slot, pl.ds(n, chunks, stride=stretch), :] = start
             state[slot, pl.ds(n, chunks, stride=stretch), :] = new
 
-    def lines(c):
-        return slice(c * stretch, c * stretch + rows)
-
-    def run(slot, unit, waits):
-        following = list(range(rows))
-        parts = jnp.zeros((rows, LANES), F32)
-        left = layers - 1
-        share = -(-rows // (left * width // block))
-        for c in range(chunks):
-            rounded[0, :, c * LANES : (c + 1) * LANES] = state[slot, lines(c), :].astype(BF16)
-        for layer in range(1, layers):
-            if waits is not None and layer < 3:
-                waits(copies[3:4] if layer == 1 else copies[4:])
-            source = rounded[(layer + 1) % 2]
-            for n in range(0, width, block):
-                product = dot(source, weights[layer - 1, :, n : n + block])
-                product = product + bias[layer : layer + 1, n : n + block]
-                gather(1 - slot, unit + 1, following[:share])
-                following = following[share:]
-                for i in range(0, block, LANES):
-                    at = lines((n + i) // LANES)
-                    new = first[slot, at, :] * product[:, i : i + LANES] + state[slot, at, :]
-                    if layer < layers - 1:
-                        state[slot, at, :] = new
-                        rounded[layer % 2, :, n + i : n + i + LANES] = new.astype(BF16)
-                    else:
-                        parts = parts + new * out_weight[:, n + i : n + i + LANES]
-        value = lane_sum(parts)
-        for k in range(ranks):
-            mine = value[k * sources : (k + 1) * sources]
-            answer[...] += jnp.where(lane == unit * ranks + k, mine, 0.0)
+    def lines(c, start, count):
+        return slice(c * stretch + start, c * stretch + start + count)
 
     def begin(s, carry):
         for k in range(ranks):
@@ -275,21 +255,74 @@
                 state[0, pl.ds(n, chunks, stride=stretch), :] = new
         return carry
 
-    lax.fori_loop(0, sources // 8, begin, 0)
-
-    def step(t, carry):
-        def waits(some):
-            @pl.when(t == 0)
-            def _():
-                for copy in some:
-                    copy.wait()
-
-        run(0, 2 * t, waits)
-        run(1, 2 * t + 1, None)
-        return carry
-
-    steps = jnp.maximum((most + 2 * ranks - 1) // (2 * ranks), 1)
-    lax.fori_loop(0, steps, step, 0)
+    halves = 2
+    half = rows // halves
+    depth = width // block
+    blocks = [(u, l, p) for u in range(units) for l in range(1, layers) for p in range(depth // 2)]
+    turns = [(*b, k) for b in blocks for k in range(depth)]
+    share = -(-rows // (((layers - 1) * depth - 2) * halves))
+    following = [list(range(rows)) for _ in range(units - 1)] + [[]]
+    parts = [[jnp.zeros((half, LANES), F32) for _ in range(halves)] for _ in range(units)]
+
+    def push(turn):
+        _, layer, p, k = turns[turn]
+        if p == 0 and k == 0 and turns[turn][0] == 0:
+            copies[2 + layer].wait()
+        for x in range(2):
+            n = (2 * p + x) * block
+            tile = weights[layer - 1, k * block : (k + 1) * block, n : n + block]
+            pltpu.matmul_push_rhs(tile, turn % 2, x)
+
+    def finish(unit, layer, p, h, x, total):
+        n = (2 * p + x) * block
+        product = pltpu.matmul_pop(total) + bias[layer : layer + 1, n : n + block]
+        gather(1 - unit % 2, unit + 1, following[unit][:share])
+        del following[unit][:share]
+        for i in range(0, block, LANES):
+            at = lines((n + i) // LANES, h * half, half)
+            new = first[unit % 2, at, :] * product[:, i : i + LANES] + state[unit % 2, at, :]
+            if layer < layers - 1:
+                state[unit % 2, at, :] = new
+                rounded[layer % 2, h * half : (h + 1) * half, n + i : n + i + LANES] = new.astype(BF16)
+            else:
+                parts[unit][h] = parts[unit][h] + new * out_weight[:, n + i : n + i + LANES]
+        if (layer, p, x) == (layers - 1, depth // 2 - 1, 1):
+            value = lane_sum(parts[unit][h])
+            for k in range(half // sources):
+                j = unit * ranks + h * half // sources + k
+                mine = value[k * sources : (k + 1) * sources]
+                answer[...] += jnp.where(lane == j, mine, 0.0)
+
+    def network(*sums):
+        def total(block_at, h, x):
+            return sums[(block_at % 2) * 4 + h * 2 + x]
+
+        greet(sums)
+        lax.fori_loop(0, sources // 8, begin, 0)
+        push(0)
+        for at, (unit, layer, p) in enumerate(blocks):
+            waiting = [] if at == 0 else [(h, x) for h in range(halves) for x in range(2)]
+            for k in range(depth):
+                turn = at * depth + k
+                if turn + 1 < len(turns):
+                    push(turn + 1)
+                for h in range(halves):
+                    own_rows = slice(h * half, (h + 1) * half)
+                    if layer == 1 and p == 0:
+                        for c in range(k * block // LANES, (k + 1) * block // LANES):
+                            entered = state[unit % 2, lines(c, h * half, half), :]
+                            rounded[0, own_rows, c * LANES : (c + 1) * LANES] = entered.astype(BF16)
+                    left = rounded[(layer + 1) % 2, own_rows, k * block : (k + 1) * block]
+                    for x in range(2):
+                        pltpu.matmul_acc_lhs(total(at, h, x), left, None if h else turn % 2)
+                for _ in range((1, 2, 1, 0)[k] if waiting else 0):
+                    h, x = waiting.pop(0)
+                    finish(*blocks[at - 1], h, x, total(at - 1, h, x))
+        for h in range(halves):
+            for x in range(2):
+                finish(*blocks[-1], h, x, total(len(blocks) - 1, h, x))
+
+    pl.run_scoped(network, *[pltpu.ACC(mxu_id=i % 2)((half, block), F32) for i in range(8)])
     logits[...] = answer[...].reshape(logits.shape)
 
 
@@ -435,11 +468,12 @@
         name="project",
         cost_estimate=pl.CostEstimate(flops=2 << 30, bytes_accessed=12 << 20, transcendentals=0),
     )(item_features, cross_weights)
-    ranks = 2
+    capacity = 3 * total // owners
+    ranks = 4
     rows = ranks * owners
     stretch = rows + 8
     answers = pl.pallas_call(
-        functools.partial(rank_kernel, ranks, 256, stretch),
+        functools.partial(rank_kernel, capacity // ranks, ranks, 256, stretch),
         out_shape=jax.ShapeDtypeStruct((owners, 1, LANES), F32),
         in_specs=[VMEM, HBM, HBM, HBM, VMEM, VMEM],
         out_specs=VMEM,

time: 61.1 us -> 60.4 us (0.989)
  starting transfers between devices: 19.7 us -> 15.4 us
  Pallas kernels: 33.7 us -> 37.4 us
    all_to_all x1, starting transfers between devices: 8.2 us -> 3.91 us  [on_device(): lax.all_to_all(answers, ('item', 'req'), split_axis=0, concat_axis=0, til...]
    pallas_call x1, Pallas kernels: 15.1 us -> 18.6 us  [on_device(): pl.pallas_call(functools.partial(rank_kernel, capacity // ranks, ranks, 2...]
where the time goes in v6:
time: 60.4 us; the launch traced here: 60.2 us
  Pallas kernels  37.4 us (62%)
  starting transfers between devices  15.4 us (25%)
  waiting for transfers between devices  6.65 us (11%)
  between operations  0.72 us (1%)
    pallas_call x1, Pallas kernels, on_device(): pl.pallas_call(functools.partial(rank_kernel, capacity // ranks, ranks, 2...  18.6 us
    all_to_all x1, starting transfers between devices, on_device(): lax.all_to_all(message, ('item', 'req'), split_axis=0, concat_axis=0, til...  11.5 us
    pallas_call x1, Pallas kernels, on_device(): pl.pallas_call(functools.partial(score_kernel, 512, looked), out_shape=ja...  9.14 us
    all_to_all x1, waiting for transfers between devices, on_device(): lax.all_to_all(message, ('item', 'req'), split_axis=0, concat_axis=0, til...  6.14 us
    pallas_call x1, Pallas kernels, on_device(): pl.pallas_call(functools.partial(project_kernel, band), out_shape=jax.Sha...  4.96 us
    all_to_all x1, starting transfers between devices, on_device(): lax.all_to_all(answers, ('item', 'req'), split_axis=0, concat_axis=0, til...  3.91 us
    pallas_call x1, Pallas kernels, on_device(): pl.pallas_call(prepare_kernel, out_shape=(jax.ShapeDtypeStruct((owners, M...  3.54 us
  transfers between devices with their start and end apart: 2, of which 2 were waited for; matrix products, arithmetic and copies ran while one was open for 0% of the time, Pallas kernels for 23%

profile of v6, /device:TPU:1, one launch (start us, length us, event | category | flops | bytes accessed | tf_op | source)
XLA Modules:
  0.0 60.2 jit_solution(2754378597454537272)
XLA Ops:
  0.6 3.5 %prepare.1 = (bf16[128,8,128]{2,1,0:T(8,128)(2,1)}, s32[512,128]{1,0:T(8,128)}) custom-call(s32[16,32]{1,0:T(8,128)} %bitcast.11, s32[1024,128]{1,0:T(8,128)} %bitcast.10, bf16[8,256]{1,0:T(8,128)(2,1)} %bitcast.13, bf16[32,256]{1,0:T(8,128)(2,1)} %user.1), custom_call_target="tpu_custom_call" | custom-call | tf_op jit(solution)/shard_map/prepare/pallas_call | solution.py:427
  4.2 11.5 %all-to-all-start = ((bf16[128,8,128]{2,1,0:T(8,128)(2,1)}), bf16[128,8,128]{2,1,0:T(8,128)(2,1)S(1)}, u32[]{:S(2)}, u32[]{:S(2)}) async-start(bf16[128,8,128]{2,1,0:T(8,128)(2,1)} %get-tuple-element.4), calls=%async_computation | async-start | bytes 524288 | tf_op jit(solution)/shard_map/all_to_all | solution.py:451
  15.7 0.0 copy-start.3
  15.7 0.0 copy-start.4
  15.7 5.0 %project.1.table_in = f32[8192,128]{1,0:T(8,128)} custom-call(bf16[1024,768]{1,0:T(8,128)(2,1)} %items_in.3, bf16[4,1024,1024]{2,1,0:T(8,128)(2,1)} %weights_in.3), custom_call_target="tpu_custom_call" | custom-call | flops 2147483648 | bytes 12582912 | tf_op jit(solution)/shard_map/project/pallas_call | solution.py:456
  20.7 6.1 %all-to-all-done.got = bf16[128,8,128]{2,1,0:T(8,128)(2,1)S(1)} async-done(((bf16[128,8,128]{2,1,0:T(8,128)(2,1)}), bf16[128,8,128]{2,1,0:T(8,128)(2,1)S(1)}, u32[]{:S(2)}, u32[]{:S(2)}) %all-to-all-start) | async-done | bytes 262176 | tf_op jit(solution)/shard_map/all_to_all | solution.py:451
  26.8 0.0 copy-done.3
  26.8 0.0 copy-done.4
  26.8 0.0 copy-start.1
  26.8 0.0 copy-start.2
  26.8 18.6 %rank.1 = f32[128,1,128]{2,1,0:T(1,128)} custom-call(bf16[128,8,128]{2,1,0:T(8,128)(2,1)S(1)} %all-to-all-done.got, f32[8192,128]{1,0:T(8,128)} %project.1.table_in, bf16[1024,768]{1,0:T(8,128)(2,1)} %items_in.3, bf16[4,1024,1024]{2,1,0:T(8,128)(2,1)} %weights_in.3, f32[4,1024]{1,0:T(4,128)S(1)} %copy-done.3, f32[1,1024]{1,0:T(1,128)S(1)} %bitcast.9), custom_call_target="tpu_custom_call" | custom-call | flops 12884901888 | bytes 10485760 | tf_op jit(solution)/shard_map/rank/pallas_call | solution.py:475
  45.4 0.0 copy-start
  45.4 3.9 %all-to-all-start.1 = ((f32[128,1,128]{2,1,0:T(1,128)}), f32[128,1,128]{2,1,0:T(1,128)S(1)}, u32[]{:S(2)}, u32[]{:S(2)}) async-start(f32[128,1,128]{2,1,0:T(1,128)} %rank.1), calls=%async_computation.1 | async-start | bytes 131072 | tf_op jit(solution)/shard_map/all_to_all | solution.py:501
  49.3 0.0 copy-done.1
  49.3 0.0 copy-done.2
  49.3 9.1 %scores.1 = f32[32,4096]{1,0:T(8,128)} custom-call(bf16[128,8,128]{2,1,0:T(8,128)(2,1)S(1)} %all-to-all-done.got, bf16[32,256]{1,0:T(8,128)(2,1)S(1)} %copy-done.1, s32[32,4096]{1,0:T(8,128)S(1)} %bitcast.8), custom_call_target="tpu_custom_call" | custom-call | flops 2147483648 | bytes 41943040 | tf_op jit(solution)/shard_map/scores/pallas_call | solution.py:503
  58.5 0.5 all-to-all-done.1.back
  59.0 0.0 copy-done
  59.0 1.2 %collect.1 = f32[16,32]{1,0:T(8,128)} custom-call(f32[128,1,128]{2,1,0:T(1,128)S(1)} %all-to-all-done.1.back, s32[512,128]{1,0:T(8,128)S(1)} %copy-done), custom_call_target="tpu_custom_call" | custom-call | tf_op jit(solution)/shard_map/collect/pallas_call | solution.py:517
Async XLA Ops:
  4.2 22.6 %all-to-all-start = ((bf16[128,8,128]{2,1,0:T(8,128)(2,1)}), bf16[128,8,128]{2,1,0:T(8,128)(2,1)S(1)}, u32[]{:S(2)}, u32[]{:S(2)}) async-start(bf16[128,8,128]{2,1,0:T(8,128)(2,1)} %get-tuple-element.4), calls=%async_computation | async-start | bytes 524288 | tf_op jit(solution)/shard_map/all_to_all | solution.py:451
  15.7 11.1 %copy-start.3 = (f32[4,1024]{1,0:T(4,128)S(1)}, f32[4,1024]{1,0:T(4,128)}, u32[]{:S(2)}) copy-start(f32[4,1024]{1,0:T(4,128)} %bias.1) | copy-start | bytes 49156
  15.7 11.1 %copy-start.4 = (f32[1024]{0:T(1024)S(1)}, f32[1024]{0:T(1024)}, u32[]{:S(2)}) copy-start(f32[1024]{0:T(1024)} %param.17) | copy-start | bytes 12292
  26.8 22.5 %copy-start.1 = (bf16[32,256]{1,0:T(8,128)(2,1)S(1)}, bf16[32,256]{1,0:T(8,128)(2,1)}, u32[]{:S(2)}) copy-start(bf16[32,256]{1,0:T(8,128)(2,1)} %user.1) | copy-start | bytes 49156
  26.8 22.5 %copy-start.2 = (s32[4096,32]{0,1:T(8,128)S(1)}, s32[4096,32]{0,1:T(8,128)}, u32[]{:S(2)}) copy-start(s32[4096,32]{0,1:T(8,128)} %param.11) | copy-start | bytes 1572868
  45.4 13.6 %copy-start = (s32[512,128]{1,0:T(8,128)S(1)}, s32[512,128]{1,0:T(8,128)}, u32[]{:S(2)}) copy-start(s32[512,128]{1,0:T(8,128)} %get-tuple-element.5.meta) | copy-start | bytes 786436
  45.4 13.6 %all-to-all-start.1 = ((f32[128,1,128]{2,1,0:T(1,128)}), f32[128,1,128]{2,1,0:T(1,128)S(1)}, u32[]{:S(2)}, u32[]{:S(2)}) async-start(f32[128,1,128]{2,1,0:T(1,128)} %rank.1), calls=%async_computation.1 | async-start | bytes 131072 | tf_op jit(solution)/shard_map/all_to_all | solution.py:501

commit v7 on v6

--- a/solution.py
+++ b/solution.py
@@ -146,14 +146,13 @@
     stretch,
     got,
     table_in,
-    items_in,
+    items,
     weights_in,
     bias,
     out_weight,
     logits,
+    early,
     table,
-    items,
-    early,
     weights,
     tiles,
     features,
@@ -173,14 +172,10 @@
     stored = items.shape[0]
     chunks = width // LANES
     own = early.shape[0] // LANES
-    copies = [
-        (weights_in.at[0, pl.ds(0, own * LANES)], early),
-        (items_in, items),
-        (table_in, table),
-    ]
+    copies = [(weights_in.at[0, pl.ds(0, own * LANES)], early), (table_in, table)]
     copies += [(weights_in.at[i], weights.at[i - 1]) for i in range(1, layers)]
     copies = [pltpu.make_async_copy(a, b, sems.at[i]) for i, (a, b) in enumerate(copies)]
-    for copy in copies:
+    for copy in copies[:2]:
         copy.start()
     reqs = lax.axis_size("req")
     tiles[...] = got[...].astype(F32).reshape(sources * MSG, LANES)
@@ -198,8 +193,8 @@
     blank = jnp.zeros((sources, LANES), F32)
     for c in range(chunks):
         people[pl.ds(c, sources, stride=chunks), :] = users[c] if c < own else blank
-    copies[0].wait()
     flat = jnp.concatenate(users, axis=1).astype(BF16)
+
     def greet(sums):
         left = jnp.concatenate([flat] * (ranks // 2), axis=0)
         for turn in range(width // block):
@@ -213,15 +208,12 @@
                 c = (turn * block + i) // LANES
                 greetings[pl.ds(c, sources, stride=chunks), :] = product[:, i : i + LANES]
 
-    copies[1].wait()
     for c in range(chunks):
         part = jnp.zeros((stored, LANES), F32)
         if c >= own:
             part = items[:, (c - own) * LANES : (c - own + 1) * LANES].astype(F32)
         features[pl.ds(c, stored, stride=chunks), :] = part
     answer[...] = jnp.zeros(answer.shape, F32)
-    fetch.wait()
-    copies[2].wait()
 
     def gather(slot, unit, some):
         values = []
@@ -267,7 +259,7 @@
     def push(turn):
         _, layer, p, k = turns[turn]
         if p == 0 and k == 0 and turns[turn][0] == 0:
-            copies[2 + layer].wait()
+            copies[1 + layer].wait()
         for x in range(2):
             n = (2 * p + x) * block
             tile = weights[layer - 1, k * block : (k + 1) * block, n : n + block]
@@ -297,7 +289,13 @@
         def total(block_at, h, x):
             return sums[(block_at % 2) * 4 + h * 2 + x]
 
+        copies[0].wait()
         greet(sums)
+        copies[2].start()
+        fetch.wait()
+        copies[1].wait()
+        for copy in copies[3:]:
+            copy.start()
         lax.fori_loop(0, sources // 8, begin, 0)
         push(0)
         for at, (unit, layer, p) in enumerate(blocks):
@@ -475,12 +473,11 @@
     answers = pl.pallas_call(
         functools.partial(rank_kernel, capacity // ranks, ranks, 256, stretch),
         out_shape=jax.ShapeDtypeStruct((owners, 1, LANES), F32),
-        in_specs=[VMEM, HBM, HBM, HBM, VMEM, VMEM],
+        in_specs=[VMEM, HBM, VMEM, HBM, VMEM, VMEM],
         out_specs=VMEM,
         scratch_shapes=[
+            pltpu.VMEM((d_user, width), BF16),
             pltpu.VMEM((lines, LANES), F32),
-            pltpu.VMEM(item_features.shape, BF16),
-            pltpu.VMEM((d_user, width), BF16),
             pltpu.VMEM((layers - 1, width, width), BF16),
             pltpu.VMEM((owners * MSG, LANES), F32),
             pltpu.VMEM((lines, LANES), F32),
@@ -492,9 +489,9 @@
             pltpu.VMEM((owners, LANES), F32),
             pltpu.VMEM((owners, LANES), I32),
             pltpu.SMEM((owners, LANES), I32),
-            pltpu.SemaphoreType.DMA((layers + 3,)),
+            pltpu.SemaphoreType.DMA((layers + 2,)),
         ],
-        compiler_params=pltpu.CompilerParams(vmem_limit_bytes=53 << 20),
+        compiler_params=pltpu.CompilerParams(vmem_limit_bytes=50 << 20),
         name="rank",
         cost_estimate=pl.CostEstimate(flops=12 << 30, bytes_accessed=10 << 20, transcendentals=0),
     )(got, table, item_features, cross_weights, cross_bias, out_weight.reshape(1, width))

time: 60.4 us -> 59.8 us (0.990)
  Pallas kernels: 37.4 us -> 36.5 us
    pallas_call x1, Pallas kernels: 18.6 us -> 17.5 us  [on_device(): pl.pallas_call(functools.partial(rank_kernel, capacity // ranks, ranks, 2...]
  transfers between devices with their start and end apart: 2 -> 2, of which waited for: 2 -> 2; matrix products, arithmetic and copies ran while one was open for 0% -> 0% of each run, Pallas kernels for 23% -> 24%
where the time goes in v7:
time: 59.8 us; the launch traced here: 59.5 us
  Pallas kernels  36.5 us (61%)
  starting transfers between devices  15.6 us (26%)
  waiting for transfers between devices  6.64 us (11%)
  between operations  0.74 us (1%)
    pallas_call x1, Pallas kernels, on_device(): pl.pallas_call(functools.partial(rank_kernel, capacity // ranks, ranks, 2...  17.5 us
    all_to_all x1, starting transfers between devices, on_device(): lax.all_to_all(message, ('item', 'req'), split_axis=0, concat_axis=0, til...  11.5 us
    pallas_call x1, Pallas kernels, on_device(): pl.pallas_call(functools.partial(score_kernel, 512, looked), out_shape=ja...  9.14 us
    all_to_all x1, waiting for transfers between devices, on_device(): lax.all_to_all(message, ('item', 'req'), split_axis=0, concat_axis=0, til...  6.02 us
    pallas_call x1, Pallas kernels, on_device(): pl.pallas_call(functools.partial(project_kernel, band), out_shape=jax.Sha...  5.06 us
    all_to_all x1, starting transfers between devices, on_device(): lax.all_to_all(answers, ('item', 'req'), split_axis=0, concat_axis=0, til...  4.13 us
    pallas_call x1, Pallas kernels, on_device(): pl.pallas_call(prepare_kernel, out_shape=(jax.ShapeDtypeStruct((owners, M...  3.54 us
  transfers between devices with their start and end apart: 2, of which 2 were waited for; matrix products, arithmetic and copies ran while one was open for 0% of the time, Pallas kernels for 24%

profile of v7, /device:TPU:1, one launch (start us, length us, event | category | flops | bytes accessed | tf_op | source)
XLA Modules:
  0.0 59.5 jit_solution(6633212242314238713)
XLA Ops:
  0.6 3.5 %prepare.1 = (bf16[128,8,128]{2,1,0:T(8,128)(2,1)}, s32[512,128]{1,0:T(8,128)}) custom-call(s32[16,32]{1,0:T(8,128)} %bitcast.11, s32[1024,128]{1,0:T(8,128)} %bitcast.10, bf16[8,256]{1,0:T(8,128)(2,1)} %bitcast.13, bf16[32,256]{1,0:T(8,128)(2,1)} %user.1), custom_call_target="tpu_custom_call" | custom-call | tf_op jit(solution)/shard_map/prepare/pallas_call | solution.py:425
  4.2 11.5 %all-to-all-start = ((bf16[128,8,128]{2,1,0:T(8,128)(2,1)}), bf16[128,8,128]{2,1,0:T(8,128)(2,1)S(1)}, u32[]{:S(2)}, u32[]{:S(2)}) async-start(bf16[128,8,128]{2,1,0:T(8,128)(2,1)} %get-tuple-element.4), calls=%async_computation | async-start | bytes 524288 | tf_op jit(solution)/shard_map/all_to_all | solution.py:449
  15.7 0.0 copy-start
  15.7 0.0 copy-start.4
  15.7 0.0 copy-start.5
  15.7 5.1 %project.1.table_in = f32[8192,128]{1,0:T(8,128)} custom-call(bf16[1024,768]{1,0:T(8,128)(2,1)} %items.1, bf16[4,1024,1024]{2,1,0:T(8,128)(2,1)} %weights_in.3), custom_call_target="tpu_custom_call" | custom-call | flops 2147483648 | bytes 12582912 | tf_op jit(solution)/shard_map/project/pallas_call | solution.py:454
  20.8 6.0 %all-to-all-done.got = bf16[128,8,128]{2,1,0:T(8,128)(2,1)S(1)} async-done(((bf16[128,8,128]{2,1,0:T(8,128)(2,1)}), bf16[128,8,128]{2,1,0:T(8,128)(2,1)S(1)}, u32[]{:S(2)}, u32[]{:S(2)}) %all-to-all-start) | async-done | bytes 262176 | tf_op jit(solution)/shard_map/all_to_all | solution.py:449
  26.8 0.0 copy-done
  26.8 0.0 copy-done.4
  26.8 0.0 copy-done.5
  26.8 0.0 copy-start.2
  26.8 0.0 copy-start.3
  26.9 17.5 %rank.1 = f32[128,1,128]{2,1,0:T(1,128)} custom-call(bf16[128,8,128]{2,1,0:T(8,128)(2,1)S(1)} %all-to-all-done.got, f32[8192,128]{1,0:T(8,128)} %project.1.table_in, bf16[1024,768]{1,0:T(8,128)(2,1)S(1)} %copy-done, bf16[4,1024,1024]{2,1,0:T(8,128)(2,1)} %weights_in.3, f32[4,1024]{1,0:T(4,128)S(1)} %copy-done.4, f32[1,1024]{1,0:T(1,128)S(1)} %bitcast.9), custom_call_target="tpu_custom_call" | custom-call | flops 12884901888 | bytes 10485760 | tf_op jit(solution)/shard_map/rank/pallas_call | solution.py:473
  44.4 0.0 copy-start.1
  44.4 4.1 %all-to-all-start.1 = ((f32[128,1,128]{2,1,0:T(1,128)}), f32[128,1,128]{2,1,0:T(1,128)S(1)}, u32[]{:S(2)}, u32[]{:S(2)}) async-start(f32[128,1,128]{2,1,0:T(1,128)} %rank.1), calls=%async_computation.1 | async-start | bytes 131072 | tf_op jit(solution)/shard_map/all_to_all | solution.py:498
  48.6 0.0 copy-done.2
  48.6 0.0 copy-done.3
  48.6 9.1 %scores.1 = f32[32,4096]{1,0:T(8,128)} custom-call(bf16[128,8,128]{2,1,0:T(8,128)(2,1)S(1)} %all-to-all-done.got, bf16[32,256]{1,0:T(8,128)(2,1)S(1)} %copy-done.2, s32[32,4096]{1,0:T(8,128)S(1)} %bitcast.8), custom_call_target="tpu_custom_call" | custom-call | flops 2147483648 | bytes 41943040 | tf_op jit(solution)/shard_map/scores/pallas_call | solution.py:500
  57.7 0.6 %all-to-all-done.1.back = f32[128,1,128]{2,1,0:T(1,128)S(1)} async-done(((f32[128,1,128]{2,1,0:T(1,128)}), f32[128,1,128]{2,1,0:T(1,128)S(1)}, u32[]{:S(2)}, u32[]{:S(2)}) %all-to-all-start.1) | async-done | bytes 65568 | tf_op jit(solution)/shard_map/all_to_all | solution.py:498
  58.3 0.0 copy-done.1
  58.3 1.2 %collect.1 = f32[16,32]{1,0:T(8,128)} custom-call(f32[128,1,128]{2,1,0:T(1,128)S(1)} %all-to-all-done.1.back, s32[512,128]{1,0:T(8,128)S(1)} %copy-done.1), custom_call_target="tpu_custom_call" | custom-call | tf_op jit(solution)/shard_map/collect/pallas_call | solution.py:514
Async XLA Ops:
  4.2 22.6 %all-to-all-start = ((bf16[128,8,128]{2,1,0:T(8,128)(2,1)}), bf16[128,8,128]{2,1,0:T(8,128)(2,1)S(1)}, u32[]{:S(2)}, u32[]{:S(2)}) async-start(bf16[128,8,128]{2,1,0:T(8,128)(2,1)} %get-tuple-element.4), calls=%async_computation | async-start | bytes 524288 | tf_op jit(solution)/shard_map/all_to_all | solution.py:449
  15.7 11.1 %copy-start = (bf16[1024,768]{1,0:T(8,128)(2,1)S(1)}, bf16[1024,768]{1,0:T(8,128)(2,1)}, u32[]{:S(2)}) copy-start(bf16[1024,768]{1,0:T(8,128)(2,1)} %items.1) | copy-start | bytes 4718596
  15.7 11.1 %copy-start.4 = (f32[4,1024]{1,0:T(4,128)S(1)}, f32[4,1024]{1,0:T(4,128)}, u32[]{:S(2)}) copy-start(f32[4,1024]{1,0:T(4,128)} %bias.1) | copy-start | bytes 49156
  15.7 11.1 %copy-start.5 = (f32[1024]{0:T(1024)S(1)}, f32[1024]{0:T(1024)}, u32[]{:S(2)}) copy-start(f32[1024]{0:T(1024)} %param.17) | copy-start | bytes 12292
  26.8 21.7 %copy-start.2 = (bf16[32,256]{1,0:T(8,128)(2,1)S(1)}, bf16[32,256]{1,0:T(8,128)(2,1)}, u32[]{:S(2)}) copy-start(bf16[32,256]{1,0:T(8,128)(2,1)} %user.1) | copy-start | bytes 49156
  26.8 21.7 %copy-start.3 = (s32[4096,32]{0,1:T(8,128)S(1)}, s32[4096,32]{0,1:T(8,128)}, u32[]{:S(2)}) copy-start(s32[4096,32]{0,1:T(8,128)} %param.11) | copy-start | bytes 1572868
  44.4 13.9 %copy-start.1 = (s32[512,128]{1,0:T(8,128)S(1)}, s32[512,128]{1,0:T(8,128)}, u32[]{:S(2)}) copy-start(s32[512,128]{1,0:T(8,128)} %get-tuple-element.5.meta) | copy-start | bytes 786436
  44.4 13.9 %all-to-all-start.1 = ((f32[128,1,128]{2,1,0:T(1,128)}), f32[128,1,128]{2,1,0:T(1,128)S(1)}, u32[]{:S(2)}, u32[]{:S(2)}) async-start(f32[128,1,128]{2,1,0:T(1,128)} %rank.1), calls=%async_computation.1 | async-start | bytes 131072 | tf_op jit(solution)/shard_map/all_to_all | solution.py:498

commit v8 on v7

--- a/solution.py
+++ b/solution.py
@@ -19,6 +19,7 @@
 WANT_ROW = 6
 HALF = 64
 CODES = 256
+PIECE = 32
 
 
 def dot(a, b, dims=(((1,), (0,)), ((), ()))):
@@ -38,7 +39,19 @@
 
 
 def prepare_kernel(
-    cand_in, place_in, codebook_in, user_in, message, meta, tiles, cand, place, codebook, user, sems
+    cand_in,
+    place_in,
+    codebook_in,
+    user_in,
+    message,
+    meta_out,
+    tiles,
+    cand,
+    place,
+    codebook,
+    user,
+    meta,
+    sems,
 ):
     pairs = ((cand_in, cand), (place_in, place), (codebook_in, codebook), (user_in, user))
     copies = [pltpu.make_async_copy(a, b, sems.at[i]) for i, (a, b) in enumerate(pairs)]
@@ -50,6 +63,45 @@
     blocks = place.shape[0]
     item = lax.axis_index("item")
     req = lax.axis_index("req")
+    copies[0].wait()
+    ids = cand[...].astype(F32)
+    spread = jnp.concatenate(
+        [jnp.broadcast_to(ids[c : c + 1, :], (requests, requests)) for c in range(cand_dev)], axis=0
+    )
+    own_request = iota((total, requests), 0) % requests
+    diagonal = own_request == iota((total, requests), 1)
+    ids = lane_sum(jnp.where(diagonal, spread, 0.0)).astype(I32)
+    where_row = as_bf16((ids >> 7) == iota((total, blocks), 1))
+    copies[1].wait()
+    stored = place[...]
+    parts = jnp.concatenate(
+        [
+            (stored & 255).astype(F32).astype(BF16),
+            ((stored >> 8) & 255).astype(F32).astype(BF16),
+            (stored >> 16).astype(F32).astype(BF16),
+        ],
+        axis=1,
+    )
+    found = dot(where_row, parts)
+    found = found[:, :LANES] + 256.0 * found[:, LANES : 2 * LANES] + 65536.0 * found[:, 2 * LANES :]
+    lane = iota((total, LANES), 1)
+    slot = lane_sum(jnp.where((ids & 127) == lane, found, 0.0)).astype(I32)
+    rows_dev = blocks * LANES // owners
+    shift = rows_dev.bit_length() - 1
+    owner = slot >> shift
+    within = slot & (rows_dev - 1)
+    hit = owner == lane
+    hits = as_bf16(hit)
+    earlier = as_bf16(iota((total, total), 1) < iota((total, total), 0))
+    rank = lane_sum(jnp.where(hit, dot(earlier, hits), 0.0)).astype(I32)
+    meta[...] = jnp.where(lane == 0, owner, rank)
+    keep = pltpu.make_async_copy(meta, meta_out, sems.at[len(copies)])
+    keep.start()
+    request = iota((total, 1), 0) % requests
+    low = (within & 255).astype(F32)
+    high = ((within >> 8) + 4 * request + 128).astype(F32)
+    entry = jnp.where(lane == rank, low, 0.0) + jnp.where(lane == rank + HALF, high, 0.0)
+    wanted = dot(hits, entry.astype(BF16), (((0,), (0,)), ((), ())))
     copies[2].wait()
     copies[3].wait()
     book = codebook[...].astype(F32)
@@ -71,45 +123,9 @@
         axis=0,
     )
     tiles[...] = jnp.broadcast_to(tile[None], (owners, MSG, LANES)).reshape(owners * MSG, LANES)
-    copies[0].wait()
-    ids = cand[...].astype(F32)
-    spread = jnp.concatenate(
-        [jnp.broadcast_to(ids[c : c + 1, :], (requests, requests)) for c in range(cand_dev)], axis=0
-    )
-    own_request = iota((total, requests), 0) % requests
-    diagonal = own_request == iota((total, requests), 1)
-    ids = lane_sum(jnp.where(diagonal, spread, 0.0)).astype(I32)
-    where_row = as_bf16((ids >> 7) == iota((total, blocks), 1))
-    copies[1].wait()
-    stored = place[...]
-    parts = jnp.concatenate(
-        [
-            (stored & 255).astype(F32).astype(BF16),
-            ((stored >> 8) & 255).astype(F32).astype(BF16),
-            (stored >> 16).astype(F32).astype(BF16),
-        ],
-        axis=1,
-    )
-    found = dot(where_row, parts)
-    found = found[:, :LANES] + 256.0 * found[:, LANES : 2 * LANES] + 65536.0 * found[:, 2 * LANES :]
-    lane = iota((total, LANES), 1)
-    slot = lane_sum(jnp.where((ids & 127) == lane, found, 0.0)).astype(I32)
-    rows_dev = blocks * LANES // owners
-    shift = rows_dev.bit_length() - 1
-    owner = slot >> shift
-    within = slot & (rows_dev - 1)
-    hit = owner == lane
-    hits = as_bf16(hit)
-    earlier = as_bf16(iota((total, total), 1) < iota((total, total), 0))
-    rank = lane_sum(jnp.where(hit, dot(earlier, hits), 0.0)).astype(I32)
-    meta[...] = jnp.where(lane == 0, owner, rank)
-    request = iota((total, 1), 0) % requests
-    low = (within & 255).astype(F32)
-    high = ((within >> 8) + 4 * request + 128).astype(F32)
-    entry = jnp.where(lane == rank, low, 0.0) + jnp.where(lane == rank + HALF, high, 0.0)
-    wanted = dot(hits, entry.astype(BF16), (((0,), (0,)), ((), ())))
     tiles[pl.ds(WANT_ROW, owners, stride=MSG), :] = wanted
     message[...] = tiles[...].reshape(owners, MSG, LANES).astype(BF16)
+    keep.wait()
 
 
 def project_kernel(band, items_in, weights_in, table, items, weights, tiles, sems):
@@ -252,7 +268,7 @@
     depth = width // block
     blocks = [(u, l, p) for u in range(units) for l in range(1, layers) for p in range(depth // 2)]
     turns = [(*b, k) for b in blocks for k in range(depth)]
-    share = -(-rows // (((layers - 1) * depth - 2) * halves))
+    share = -(-rows // (((layers - 1) * depth // 2 - 1) * depth))
     following = [list(range(rows)) for _ in range(units - 1)] + [[]]
     parts = [[jnp.zeros((half, LANES), F32) for _ in range(halves)] for _ in range(units)]
 
@@ -268,8 +284,6 @@
     def finish(unit, layer, p, h, x, total):
         n = (2 * p + x) * block
         product = pltpu.matmul_pop(total) + bias[layer : layer + 1, n : n + block]
-        gather(1 - unit % 2, unit + 1, following[unit][:share])
-        del following[unit][:share]
         for i in range(0, block, LANES):
             at = lines((n + i) // LANES, h * half, half)
             new = first[unit % 2, at, :] * product[:, i : i + LANES] + state[unit % 2, at, :]
@@ -313,6 +327,9 @@
                     left = rounded[(layer + 1) % 2, own_rows, k * block : (k + 1) * block]
                     for x in range(2):
                         pltpu.matmul_acc_lhs(total(at, h, x), left, None if h else turn % 2)
+                if (layer, p) != (1, 0):
+                    gather(1 - unit % 2, unit + 1, following[unit][:share])
+                    del following[unit][:share]
                 for _ in range((1, 2, 1, 0)[k] if waiting else 0):
                     h, x = waiting.pop(0)
                     finish(*blocks[at - 1], h, x, total(at - 1, h, x))
@@ -392,12 +409,14 @@
     lane = iota((total, owners), 1)
     answers = back[...].reshape(owners, LANES)
     pick = as_bf16(meta[:, 0:1] == lane)
-    top = answers.astype(BF16)
-    rest = answers - top.astype(F32)
-    middle = rest.astype(BF16)
-    last = (rest - middle.astype(F32)).astype(BF16)
-    rows = dot(pick, top) + dot(pick, middle) + dot(pick, last)
-    value = lane_sum(jnp.where(meta[:, 1:2] == lane, rows, 0.0))
+    top = answers.astype(BF16).astype(F32)
+    rest = answers - top
+    middle = rest.astype(BF16).astype(F32)
+    last = rest - middle
+    pieces = top + pltpu.roll(middle, PIECE, axis=1) + pltpu.roll(last, 2 * PIECE, axis=1)
+    rows = dot(pick, pieces.astype(BF16))
+    mine = (lane % PIECE == meta[:, 1:2]) & (lane < 3 * PIECE)
+    value = lane_sum(jnp.where(mine, rows, 0.0))
     diagonal = iota((total, requests), 0) % requests == iota((total, requests), 1)
     spread = jnp.where(diagonal, value, 0.0)
     logits[...] = jnp.sum(spread.reshape(cand_dev, requests, requests), axis=1)
@@ -429,14 +448,15 @@
             jax.ShapeDtypeStruct((total, LANES), I32),
         ),
         in_specs=[HBM] * 4,
-        out_specs=(VMEM, VMEM),
+        out_specs=(VMEM, HBM),
         scratch_shapes=[
             pltpu.VMEM((owners * MSG, LANES), F32),
             pltpu.VMEM((cand_dev, requests), I32),
             pltpu.VMEM((item_place.shape[0] // LANES, LANES), I32),
             pltpu.VMEM(codebooks.shape[:0:-1], BF16),
             pltpu.VMEM(user_emb.shape, BF16),
-            pltpu.SemaphoreType.DMA((4,)),
+            pltpu.VMEM((total, LANES), I32),
+            pltpu.SemaphoreType.DMA((5,)),
         ],
         compiler_params=whole,
         name="prepare",

time: 59.8 us -> 60 us (level)
  no operation moved by 1% of the time
where the time goes in v8:
time: 60 us; the launch traced here: 59.8 us
  Pallas kernels  36.8 us (61%)
  starting transfers between devices  15.6 us (26%)
  waiting for transfers between devices  6.64 us (11%)
  between operations  0.74 us (1%)
    pallas_call x1, Pallas kernels, on_device(): pl.pallas_call(functools.partial(rank_kernel, capacity // ranks, ranks, 2...  17.6 us
    all_to_all x1, starting transfers between devices, on_device(): lax.all_to_all(message, ('item', 'req'), split_axis=0, concat_axis=0, til...  11.5 us
    pallas_call x1, Pallas kernels, on_device(): pl.pallas_call(functools.partial(score_kernel, 512, looked), out_shape=ja...  9.14 us
    all_to_all x1, waiting for transfers between devices, on_device(): lax.all_to_all(message, ('item', 'req'), split_axis=0, concat_axis=0, til...  6.02 us
    pallas_call x1, Pallas kernels, on_device(): pl.pallas_call(functools.partial(project_kernel, band), out_shape=jax.Sha...  5.06 us
    all_to_all x1, starting transfers between devices, on_device(): lax.all_to_all(answers, ('item', 'req'), split_axis=0, concat_axis=0, til...  4.12 us
    pallas_call x1, Pallas kernels, on_device(): pl.pallas_call(prepare_kernel, out_shape=(jax.ShapeDtypeStruct((owners, M...  3.83 us
  transfers between devices with their start and end apart: 2, of which 2 were waited for; matrix products, arithmetic and copies ran while one was open for 0% of the time, Pallas kernels for 24%

profile of v8, /device:TPU:1, one launch (start us, length us, event | category | flops | bytes accessed | tf_op | source)
XLA Modules:
  0.0 59.8 jit_solution(15279429412911003515)
XLA Ops:
  0.6 3.8 %prepare.1 = (bf16[128,8,128]{2,1,0:T(8,128)(2,1)}, s32[512,128]{1,0:T(8,128)}) custom-call(s32[16,32]{1,0:T(8,128)} %bitcast.11, s32[1024,128]{1,0:T(8,128)} %bitcast.10, bf16[8,256]{1,0:T(8,128)(2,1)} %bitcast.13, bf16[32,256]{1,0:T(8,128)(2,1)} %user.1), custom_call_target="tpu_custom_call" | custom-call | tf_op jit(solution)/shard_map/prepare/pallas_call | solution.py:444
  4.5 11.5 %all-to-all-start = ((bf16[128,8,128]{2,1,0:T(8,128)(2,1)}), bf16[128,8,128]{2,1,0:T(8,128)(2,1)S(1)}, u32[]{:S(2)}, u32[]{:S(2)}) async-start(bf16[128,8,128]{2,1,0:T(8,128)(2,1)} %get-tuple-element.4), calls=%async_computation | async-start | bytes 524288 | tf_op jit(solution)/shard_map/all_to_all | solution.py:469
  16.0 0.0 copy-start
  16.0 0.0 copy-start.4
  16.0 0.0 copy-start.5
  16.0 5.1 %project.1.table_in = f32[8192,128]{1,0:T(8,128)} custom-call(bf16[1024,768]{1,0:T(8,128)(2,1)} %items.1, bf16[4,1024,1024]{2,1,0:T(8,128)(2,1)} %weights_in.3), custom_call_target="tpu_custom_call" | custom-call | flops 2147483648 | bytes 12582912 | tf_op jit(solution)/shard_map/project/pallas_call | solution.py:474
  21.1 6.0 %all-to-all-done.got = bf16[128,8,128]{2,1,0:T(8,128)(2,1)S(1)} async-done(((bf16[128,8,128]{2,1,0:T(8,128)(2,1)}), bf16[128,8,128]{2,1,0:T(8,128)(2,1)S(1)}, u32[]{:S(2)}, u32[]{:S(2)}) %all-to-all-start) | async-done | bytes 262176 | tf_op jit(solution)/shard_map/all_to_all | solution.py:469
  27.1 0.0 copy-done
  27.1 0.0 copy-done.4
  27.1 0.0 copy-done.5
  27.1 0.0 copy-start.2
  27.1 0.0 copy-start.3
  27.1 17.6 %rank.1 = f32[128,1,128]{2,1,0:T(1,128)} custom-call(bf16[128,8,128]{2,1,0:T(8,128)(2,1)S(1)} %all-to-all-done.got, f32[8192,128]{1,0:T(8,128)} %project.1.table_in, bf16[1024,768]{1,0:T(8,128)(2,1)S(1)} %copy-done, bf16[4,1024,1024]{2,1,0:T(8,128)(2,1)} %weights_in.3, f32[4,1024]{1,0:T(4,128)S(1)} %copy-done.4, f32[1,1024]{1,0:T(1,128)S(1)} %bitcast.9), custom_call_target="tpu_custom_call" | custom-call | flops 12884901888 | bytes 10485760 | tf_op jit(solution)/shard_map/rank/pallas_call | solution.py:493
  44.8 0.0 copy-start.1
  44.8 4.1 %all-to-all-start.1 = ((f32[128,1,128]{2,1,0:T(1,128)}), f32[128,1,128]{2,1,0:T(1,128)S(1)}, u32[]{:S(2)}, u32[]{:S(2)}) async-start(f32[128,1,128]{2,1,0:T(1,128)} %rank.1), calls=%async_computation.1 | async-start | bytes 131072 | tf_op jit(solution)/shard_map/all_to_all | solution.py:518
  48.9 0.0 copy-done.2
  48.9 0.0 copy-done.3
  48.9 9.1 %scores.1 = f32[32,4096]{1,0:T(8,128)} custom-call(bf16[128,8,128]{2,1,0:T(8,128)(2,1)S(1)} %all-to-all-done.got, bf16[32,256]{1,0:T(8,128)(2,1)S(1)} %copy-done.2, s32[32,4096]{1,0:T(8,128)S(1)} %bitcast.8), custom_call_target="tpu_custom_call" | custom-call | flops 2147483648 | bytes 41943040 | tf_op jit(solution)/shard_map/scores/pallas_call | solution.py:520
  58.1 0.6 %all-to-all-done.1.back = f32[128,1,128]{2,1,0:T(1,128)S(1)} async-done(((f32[128,1,128]{2,1,0:T(1,128)}), f32[128,1,128]{2,1,0:T(1,128)S(1)}, u32[]{:S(2)}, u32[]{:S(2)}) %all-to-all-start.1) | async-done | bytes 65568 | tf_op jit(solution)/shard_map/all_to_all | solution.py:518
  58.7 0.0 copy-done.1
  58.7 1.1 %collect.1 = f32[16,32]{1,0:T(8,128)} custom-call(f32[128,1,128]{2,1,0:T(1,128)S(1)} %all-to-all-done.1.back, s32[512,128]{1,0:T(8,128)S(1)} %copy-done.1), custom_call_target="tpu_custom_call" | custom-call | tf_op jit(solution)/shard_map/collect/pallas_call | solution.py:534
Async XLA Ops:
  4.5 22.6 %all-to-all-start = ((bf16[128,8,128]{2,1,0:T(8,128)(2,1)}), bf16[128,8,128]{2,1,0:T(8,128)(2,1)S(1)}, u32[]{:S(2)}, u32[]{:S(2)}) async-start(bf16[128,8,128]{2,1,0:T(8,128)(2,1)} %get-tuple-element.4), calls=%async_computation | async-start | bytes 524288 | tf_op jit(solution)/shard_map/all_to_all | solution.py:469
  16.0 11.1 %copy-start = (bf16[1024,768]{1,0:T(8,128)(2,1)S(1)}, bf16[1024,768]{1,0:T(8,128)(2,1)}, u32[]{:S(2)}) copy-start(bf16[1024,768]{1,0:T(8,128)(2,1)} %items.1) | copy-start | bytes 4718596
  16.0 11.1 %copy-start.4 = (f32[4,1024]{1,0:T(4,128)S(1)}, f32[4,1024]{1,0:T(4,128)}, u32[]{:S(2)}) copy-start(f32[4,1024]{1,0:T(4,128)} %bias.1) | copy-start | bytes 49156
  16.0 11.1 %copy-start.5 = (f32[1024]{0:T(1024)S(1)}, f32[1024]{0:T(1024)}, u32[]{:S(2)}) copy-start(f32[1024]{0:T(1024)} %param.17) | copy-start | bytes 12292
  27.1 21.8 %copy-start.2 = (bf16[32,256]{1,0:T(8,128)(2,1)S(1)}, bf16[32,256]{1,0:T(8,128)(2,1)}, u32[]{:S(2)}) copy-start(bf16[32,256]{1,0:T(8,128)(2,1)} %user.1) | copy-start | bytes 49156
  27.1 21.8 %copy-start.3 = (s32[4096,32]{0,1:T(8,128)S(1)}, s32[4096,32]{0,1:T(8,128)}, u32[]{:S(2)}) copy-start(s32[4096,32]{0,1:T(8,128)} %param.11) | copy-start | bytes 1572868
  44.8 13.9 %copy-start.1 = (s32[512,128]{1,0:T(8,128)S(1)}, s32[512,128]{1,0:T(8,128)}, u32[]{:S(2)}) copy-start(s32[512,128]{1,0:T(8,128)} %get-tuple-element.5.meta) | copy-start | bytes 786436
  44.8 13.9 %all-to-all-start.1 = ((f32[128,1,128]{2,1,0:T(1,128)}), f32[128,1,128]{2,1,0:T(1,128)S(1)}, u32[]{:S(2)}, u32[]{:S(2)}) async-start(f32[128,1,128]{2,1,0:T(1,128)} %rank.1), calls=%async_computation.1 | async-start | bytes 131072 | tf_op jit(solution)/shard_map/all_to_all | solution.py:518

commit v9 on v8

--- a/solution.py
+++ b/solution.py
@@ -39,31 +39,20 @@
 
 
 def prepare_kernel(
-    cand_in,
-    place_in,
-    codebook_in,
-    user_in,
-    message,
-    meta_out,
-    tiles,
-    cand,
-    place,
-    codebook,
-    user,
-    meta,
-    sems,
+    cand_in, place_in, codebook_in, user_in, message, meta, tiles, cand, place, codebook, user, sems
 ):
     pairs = ((cand_in, cand), (place_in, place), (codebook_in, codebook), (user_in, user))
     copies = [pltpu.make_async_copy(a, b, sems.at[i]) for i, (a, b) in enumerate(pairs)]
     for copy in copies:
         copy.start()
+    for copy in copies:
+        copy.wait()
     cand_dev, requests = cand.shape
     total = cand_dev * requests
     owners = message.shape[0]
     blocks = place.shape[0]
     item = lax.axis_index("item")
     req = lax.axis_index("req")
-    copies[0].wait()
     ids = cand[...].astype(F32)
     spread = jnp.concatenate(
         [jnp.broadcast_to(ids[c : c + 1, :], (requests, requests)) for c in range(cand_dev)], axis=0
@@ -72,7 +61,6 @@
     diagonal = own_request == iota((total, requests), 1)
     ids = lane_sum(jnp.where(diagonal, spread, 0.0)).astype(I32)
     where_row = as_bf16((ids >> 7) == iota((total, blocks), 1))
-    copies[1].wait()
     stored = place[...]
     parts = jnp.concatenate(
         [
@@ -95,15 +83,11 @@
     earlier = as_bf16(iota((total, total), 1) < iota((total, total), 0))
     rank = lane_sum(jnp.where(hit, dot(earlier, hits), 0.0)).astype(I32)
     meta[...] = jnp.where(lane == 0, owner, rank)
-    keep = pltpu.make_async_copy(meta, meta_out, sems.at[len(copies)])
-    keep.start()
     request = iota((total, 1), 0) % requests
     low = (within & 255).astype(F32)
     high = ((within >> 8) + 4 * request + 128).astype(F32)
     entry = jnp.where(lane == rank, low, 0.0) + jnp.where(lane == rank + HALF, high, 0.0)
     wanted = dot(hits, entry.astype(BF16), (((0,), (0,)), ((), ())))
-    copies[2].wait()
-    copies[3].wait()
     book = codebook[...].astype(F32)
     sub = iota(book.shape, 0)
     first = jnp.sum(jnp.where(sub == 2 * req, book, 0.0), axis=0, keepdims=True)
@@ -125,7 +109,6 @@
     tiles[...] = jnp.broadcast_to(tile[None], (owners, MSG, LANES)).reshape(owners * MSG, LANES)
     tiles[pl.ds(WANT_ROW, owners, stride=MSG), :] = wanted
     message[...] = tiles[...].reshape(owners, MSG, LANES).astype(BF16)
-    keep.wait()
 
 
 def project_kernel(band, items_in, weights_in, table, items, weights, tiles, sems):
@@ -448,15 +431,14 @@
             jax.ShapeDtypeStruct((total, LANES), I32),
         ),
         in_specs=[HBM] * 4,
-        out_specs=(VMEM, HBM),
+        out_specs=(VMEM, VMEM),
         scratch_shapes=[
             pltpu.VMEM((owners * MSG, LANES), F32),
             pltpu.VMEM((cand_dev, requests), I32),
             pltpu.VMEM((item_place.shape[0] // LANES, LANES), I32),
             pltpu.VMEM(codebooks.shape[:0:-1], BF16),
             pltpu.VMEM(user_emb.shape, BF16),
-            pltpu.VMEM((total, LANES), I32),
-            pltpu.SemaphoreType.DMA((5,)),
+            pltpu.SemaphoreType.DMA((4,)),
         ],
         compiler_params=whole,
         name="prepare",

time: 60 us -> 59.6 us (level)
  no operation moved by 1% of the time
where the time goes in v9:
time: 59.6 us; the launch traced here: 59.4 us
  Pallas kernels  36.4 us (61%)
  starting transfers between devices  15.6 us (26%)
  waiting for transfers between devices  6.64 us (11%)
  between operations  0.74 us (1%)
    pallas_call x1, Pallas kernels, on_device(): pl.pallas_call(functools.partial(rank_kernel, capacity // ranks, ranks, 2...  17.6 us
    all_to_all x1, starting transfers between devices, on_device(): lax.all_to_all(message, ('item', 'req'), split_axis=0, concat_axis=0, til...  11.5 us
    pallas_call x1, Pallas kernels, on_device(): pl.pallas_call(functools.partial(score_kernel, 512, looked), out_shape=ja...  9.14 us
    all_to_all x1, waiting for transfers between devices, on_device(): lax.all_to_all(message, ('item', 'req'), split_axis=0, concat_axis=0, til...  6.02 us
    pallas_call x1, Pallas kernels, on_device(): pl.pallas_call(functools.partial(project_kernel, band), out_shape=jax.Sha...  5.06 us
    all_to_all x1, starting transfers between devices, on_device(): lax.all_to_all(answers, ('item', 'req'), split_axis=0, concat_axis=0, til...  4.1 us
    pallas_call x1, Pallas kernels, on_device(): pl.pallas_call(prepare_kernel, out_shape=(jax.ShapeDtypeStruct((owners, M...  3.39 us
  transfers between devices with their start and end apart: 2, of which 2 were waited for; matrix products, arithmetic and copies ran while one was open for 0% of the time, Pallas kernels for 24%

profile of v9, /device:TPU:1, one launch (start us, length us, event | category | flops | bytes accessed | tf_op | source)
XLA Modules:
  0.0 59.4 jit_solution(11752842130068747944)
XLA Ops:
  0.6 3.4 %prepare.1 = (bf16[128,8,128]{2,1,0:T(8,128)(2,1)}, s32[512,128]{1,0:T(8,128)}) custom-call(s32[16,32]{1,0:T(8,128)} %bitcast.11, s32[1024,128]{1,0:T(8,128)} %bitcast.10, bf16[8,256]{1,0:T(8,128)(2,1)} %bitcast.13, bf16[32,256]{1,0:T(8,128)(2,1)} %user.1), custom_call_target="tpu_custom_call" | custom-call | tf_op jit(solution)/shard_map/prepare/pallas_call | solution.py:427
  4.0 11.5 %all-to-all-start = ((bf16[128,8,128]{2,1,0:T(8,128)(2,1)}), bf16[128,8,128]{2,1,0:T(8,128)(2,1)S(1)}, u32[]{:S(2)}, u32[]{:S(2)}) async-start(bf16[128,8,128]{2,1,0:T(8,128)(2,1)} %get-tuple-element.4), calls=%async_computation | async-start | bytes 524288 | tf_op jit(solution)/shard_map/all_to_all | solution.py:451
  15.5 0.0 copy-start
  15.6 0.0 copy-start.4
  15.6 0.0 copy-start.5
  15.6 5.1 %project.1.table_in = f32[8192,128]{1,0:T(8,128)} custom-call(bf16[1024,768]{1,0:T(8,128)(2,1)} %items.1, bf16[4,1024,1024]{2,1,0:T(8,128)(2,1)} %weights_in.3), custom_call_target="tpu_custom_call" | custom-call | flops 2147483648 | bytes 12582912 | tf_op jit(solution)/shard_map/project/pallas_call | solution.py:456
  20.6 6.0 %all-to-all-done.got = bf16[128,8,128]{2,1,0:T(8,128)(2,1)S(1)} async-done(((bf16[128,8,128]{2,1,0:T(8,128)(2,1)}), bf16[128,8,128]{2,1,0:T(8,128)(2,1)S(1)}, u32[]{:S(2)}, u32[]{:S(2)}) %all-to-all-start) | async-done | bytes 262176 | tf_op jit(solution)/shard_map/all_to_all | solution.py:451
  26.7 0.0 copy-done
  26.7 0.0 copy-done.4
  26.7 0.0 copy-done.5
  26.7 0.0 copy-start.2
  26.7 0.0 copy-start.3
  26.7 17.6 %rank.1 = f32[128,1,128]{2,1,0:T(1,128)} custom-call(bf16[128,8,128]{2,1,0:T(8,128)(2,1)S(1)} %all-to-all-done.got, f32[8192,128]{1,0:T(8,128)} %project.1.table_in, bf16[1024,768]{1,0:T(8,128)(2,1)S(1)} %copy-done, bf16[4,1024,1024]{2,1,0:T(8,128)(2,1)} %weights_in.3, f32[4,1024]{1,0:T(4,128)S(1)} %copy-done.4, f32[1,1024]{1,0:T(1,128)S(1)} %bitcast.9), custom_call_target="tpu_custom_call" | custom-call | flops 12884901888 | bytes 10485760 | tf_op jit(solution)/shard_map/rank/pallas_call | solution.py:475
  44.3 0.0 copy-start.1
  44.3 4.1 %all-to-all-start.1 = ((f32[128,1,128]{2,1,0:T(1,128)}), f32[128,1,128]{2,1,0:T(1,128)S(1)}, u32[]{:S(2)}, u32[]{:S(2)}) async-start(f32[128,1,128]{2,1,0:T(1,128)} %rank.1), calls=%async_computation.1 | async-start | bytes 131072 | tf_op jit(solution)/shard_map/all_to_all | solution.py:500
  48.5 0.0 copy-done.2
  48.5 0.0 copy-done.3
  48.5 9.1 %scores.1 = f32[32,4096]{1,0:T(8,128)} custom-call(bf16[128,8,128]{2,1,0:T(8,128)(2,1)S(1)} %all-to-all-done.got, bf16[32,256]{1,0:T(8,128)(2,1)S(1)} %copy-done.2, s32[32,4096]{1,0:T(8,128)S(1)} %bitcast.8), custom_call_target="tpu_custom_call" | custom-call | flops 2147483648 | bytes 41943040 | tf_op jit(solution)/shard_map/scores/pallas_call | solution.py:502
  57.6 0.6 %all-to-all-done.1.back = f32[128,1,128]{2,1,0:T(1,128)S(1)} async-done(((f32[128,1,128]{2,1,0:T(1,128)}), f32[128,1,128]{2,1,0:T(1,128)S(1)}, u32[]{:S(2)}, u32[]{:S(2)}) %all-to-all-start.1) | async-done | bytes 65568 | tf_op jit(solution)/shard_map/all_to_all | solution.py:500
  58.2 0.0 copy-done.1
  58.2 1.1 %collect.1 = f32[16,32]{1,0:T(8,128)} custom-call(f32[128,1,128]{2,1,0:T(1,128)S(1)} %all-to-all-done.1.back, s32[512,128]{1,0:T(8,128)S(1)} %copy-done.1), custom_call_target="tpu_custom_call" | custom-call | tf_op jit(solution)/shard_map/collect/pallas_call | solution.py:516
Async XLA Ops:
  4.0 22.6 %all-to-all-start = ((bf16[128,8,128]{2,1,0:T(8,128)(2,1)}), bf16[128,8,128]{2,1,0:T(8,128)(2,1)S(1)}, u32[]{:S(2)}, u32[]{:S(2)}) async-start(bf16[128,8,128]{2,1,0:T(8,128)(2,1)} %get-tuple-element.4), calls=%async_computation | async-start | bytes 524288 | tf_op jit(solution)/shard_map/all_to_all | solution.py:451
  15.5 11.1 %copy-start = (bf16[1024,768]{1,0:T(8,128)(2,1)S(1)}, bf16[1024,768]{1,0:T(8,128)(2,1)}, u32[]{:S(2)}) copy-start(bf16[1024,768]{1,0:T(8,128)(2,1)} %items.1) | copy-start | bytes 4718596
  15.6 11.1 %copy-start.4 = (f32[4,1024]{1,0:T(4,128)S(1)}, f32[4,1024]{1,0:T(4,128)}, u32[]{:S(2)}) copy-start(f32[4,1024]{1,0:T(4,128)} %bias.1) | copy-start | bytes 49156
  15.6 11.1 %copy-start.5 = (f32[1024]{0:T(1024)S(1)}, f32[1024]{0:T(1024)}, u32[]{:S(2)}) copy-start(f32[1024]{0:T(1024)} %param.17) | copy-start | bytes 12292
  26.7 21.8 %copy-start.2 = (bf16[32,256]{1,0:T(8,128)(2,1)S(1)}, bf16[32,256]{1,0:T(8,128)(2,1)}, u32[]{:S(2)}) copy-start(bf16[32,256]{1,0:T(8,128)(2,1)} %user.1) | copy-start | bytes 49156
  26.7 21.8 %copy-start.3 = (s32[4096,32]{0,1:T(8,128)S(1)}, s32[4096,32]{0,1:T(8,128)}, u32[]{:S(2)}) copy-start(s32[4096,32]{0,1:T(8,128)} %param.11) | copy-start | bytes 1572868
  44.3 13.9 %copy-start.1 = (s32[512,128]{1,0:T(8,128)S(1)}, s32[512,128]{1,0:T(8,128)}, u32[]{:S(2)}) copy-start(s32[512,128]{1,0:T(8,128)} %get-tuple-element.5.meta) | copy-start | bytes 786436
  44.3 13.9 %all-to-all-start.1 = ((f32[128,1,128]{2,1,0:T(1,128)}), f32[128,1,128]{2,1,0:T(1,128)S(1)}, u32[]{:S(2)}, u32[]{:S(2)}) async-start(f32[128,1,128]{2,1,0:T(1,128)} %rank.1), calls=%async_computation.1 | async-start | bytes 131072 | tf_op jit(solution)/shard_map/all_to_all | solution.py:500

commit v10 on v9

--- a/solution.py
+++ b/solution.py
@@ -452,7 +452,7 @@
     stored, features = item_features.shape
     chunks = width // LANES
     lines = stored * chunks
-    band = stored // 4
+    band = stored // 8
     table = pl.pallas_call(
         functools.partial(project_kernel, band),
         out_shape=jax.ShapeDtypeStruct((lines, LANES), F32),

time: 59.6 us -> 59.6 us (level)
  transfers between devices with their start and end apart: 2 -> 2, of which waited for: 2 -> 2; matrix products, arithmetic and copies ran while one was open for 0% -> 0% of each run, Pallas kernels for 24% -> 23%
where the time goes in v10:
time: 59.6 us; the launch traced here: 59.4 us
  Pallas kernels  36 us (60%)
  starting transfers between devices  15.6 us (26%)
  waiting for transfers between devices  6.94 us (12%)
  between operations  0.74 us (1%)
    pallas_call x1, Pallas kernels, on_device(): pl.pallas_call(functools.partial(rank_kernel, capacity // ranks, ranks, 2...  17.6 us
    all_to_all x1, starting transfers between devices, on_device(): lax.all_to_all(message, ('item', 'req'), split_axis=0, concat_axis=0, til...  11.5 us
    pallas_call x1, Pallas kernels, on_device(): pl.pallas_call(functools.partial(score_kernel, 512, looked), out_shape=ja...  9.14 us
    all_to_all x1, waiting for transfers between devices, on_device(): lax.all_to_all(message, ('item', 'req'), split_axis=0, concat_axis=0, til...  6.32 us
    pallas_call x1, Pallas kernels, on_device(): pl.pallas_call(functools.partial(project_kernel, band), out_shape=jax.Sha...  4.76 us
    all_to_all x1, starting transfers between devices, on_device(): lax.all_to_all(answers, ('item', 'req'), split_axis=0, concat_axis=0, til...  4.11 us
    pallas_call x1, Pallas kernels, on_device(): pl.pallas_call(prepare_kernel, out_shape=(jax.ShapeDtypeStruct((owners, M...  3.39 us
  transfers between devices with their start and end apart: 2, of which 2 were waited for; matrix products, arithmetic and copies ran while one was open for 0% of the time, Pallas kernels for 23%

profile of v10, /device:TPU:1, one launch (start us, length us, event | category | flops | bytes accessed | tf_op | source)
XLA Modules:
  0.0 59.4 jit_solution(7382026157996045290)
XLA Ops:
  0.6 3.4 %prepare.1 = (bf16[128,8,128]{2,1,0:T(8,128)(2,1)}, s32[512,128]{1,0:T(8,128)}) custom-call(s32[16,32]{1,0:T(8,128)} %bitcast.11, s32[1024,128]{1,0:T(8,128)} %bitcast.10, bf16[8,256]{1,0:T(8,128)(2,1)} %bitcast.13, bf16[32,256]{1,0:T(8,128)(2,1)} %user.1), custom_call_target="tpu_custom_call" | custom-call | tf_op jit(solution)/shard_map/prepare/pallas_call | solution.py:427
  4.0 11.5 %all-to-all-start = ((bf16[128,8,128]{2,1,0:T(8,128)(2,1)}), bf16[128,8,128]{2,1,0:T(8,128)(2,1)S(1)}, u32[]{:S(2)}, u32[]{:S(2)}) async-start(bf16[128,8,128]{2,1,0:T(8,128)(2,1)} %get-tuple-element.4), calls=%async_computation | async-start | bytes 524288 | tf_op jit(solution)/shard_map/all_to_all | solution.py:451
  15.5 0.0 copy-start
  15.6 0.0 copy-start.4
  15.6 0.0 copy-start.5
  15.6 4.8 %project.1.table_in = f32[8192,128]{1,0:T(8,128)} custom-call(bf16[1024,768]{1,0:T(8,128)(2,1)} %items.1, bf16[4,1024,1024]{2,1,0:T(8,128)(2,1)} %weights_in.3), custom_call_target="tpu_custom_call" | custom-call | flops 2147483648 | bytes 12582912 | tf_op jit(solution)/shard_map/project/pallas_call | solution.py:456
  20.3 6.3 %all-to-all-done.got = bf16[128,8,128]{2,1,0:T(8,128)(2,1)S(1)} async-done(((bf16[128,8,128]{2,1,0:T(8,128)(2,1)}), bf16[128,8,128]{2,1,0:T(8,128)(2,1)S(1)}, u32[]{:S(2)}, u32[]{:S(2)}) %all-to-all-start) | async-done | bytes 262176 | tf_op jit(solution)/shard_map/all_to_all | solution.py:451
  26.7 0.0 copy-done
  26.7 0.0 copy-done.4
  26.7 0.0 copy-done.5
  26.7 0.0 copy-start.2
  26.7 0.0 copy-start.3
  26.7 17.6 %rank.1 = f32[128,1,128]{2,1,0:T(1,128)} custom-call(bf16[128,8,128]{2,1,0:T(8,128)(2,1)S(1)} %all-to-all-done.got, f32[8192,128]{1,0:T(8,128)} %project.1.table_in, bf16[1024,768]{1,0:T(8,128)(2,1)S(1)} %copy-done, bf16[4,1024,1024]{2,1,0:T(8,128)(2,1)} %weights_in.3, f32[4,1024]{1,0:T(4,128)S(1)} %copy-done.4, f32[1,1024]{1,0:T(1,128)S(1)} %bitcast.9), custom_call_target="tpu_custom_call" | custom-call | flops 12884901888 | bytes 10485760 | tf_op jit(solution)/shard_map/rank/pallas_call | solution.py:475
  44.3 0.0 copy-start.1
  44.3 4.1 %all-to-all-start.1 = ((f32[128,1,128]{2,1,0:T(1,128)}), f32[128,1,128]{2,1,0:T(1,128)S(1)}, u32[]{:S(2)}, u32[]{:S(2)}) async-start(f32[128,1,128]{2,1,0:T(1,128)} %rank.1), calls=%async_computation.1 | async-start | bytes 131072 | tf_op jit(solution)/shard_map/all_to_all | solution.py:500
  48.5 0.0 copy-done.2
  48.5 0.0 copy-done.3
  48.5 9.1 %scores.1 = f32[32,4096]{1,0:T(8,128)} custom-call(bf16[128,8,128]{2,1,0:T(8,128)(2,1)S(1)} %all-to-all-done.got, bf16[32,256]{1,0:T(8,128)(2,1)S(1)} %copy-done.2, s32[32,4096]{1,0:T(8,128)S(1)} %bitcast.8), custom_call_target="tpu_custom_call" | custom-call | flops 2147483648 | bytes 41943040 | tf_op jit(solution)/shard_map/scores/pallas_call | solution.py:502
  57.6 0.6 %all-to-all-done.1.back = f32[128,1,128]{2,1,0:T(1,128)S(1)} async-done(((f32[128,1,128]{2,1,0:T(1,128)}), f32[128,1,128]{2,1,0:T(1,128)S(1)}, u32[]{:S(2)}, u32[]{:S(2)}) %all-to-all-start.1) | async-done | bytes 65568 | tf_op jit(solution)/shard_map/all_to_all | solution.py:500
  58.2 0.0 copy-done.1
  58.2 1.1 %collect.1 = f32[16,32]{1,0:T(8,128)} custom-call(f32[128,1,128]{2,1,0:T(1,128)S(1)} %all-to-all-done.1.back, s32[512,128]{1,0:T(8,128)S(1)} %copy-done.1), custom_call_target="tpu_custom_call" | custom-call | tf_op jit(solution)/shard_map/collect/pallas_call | solution.py:516
Async XLA Ops:
  4.0 22.6 %all-to-all-start = ((bf16[128,8,128]{2,1,0:T(8,128)(2,1)}), bf16[128,8,128]{2,1,0:T(8,128)(2,1)S(1)}, u32[]{:S(2)}, u32[]{:S(2)}) async-start(bf16[128,8,128]{2,1,0:T(8,128)(2,1)} %get-tuple-element.4), calls=%async_computation | async-start | bytes 524288 | tf_op jit(solution)/shard_map/all_to_all | solution.py:451
  15.5 11.1 %copy-start = (bf16[1024,768]{1,0:T(8,128)(2,1)S(1)}, bf16[1024,768]{1,0:T(8,128)(2,1)}, u32[]{:S(2)}) copy-start(bf16[1024,768]{1,0:T(8,128)(2,1)} %items.1) | copy-start | bytes 4718596
  15.6 11.1 %copy-start.4 = (f32[4,1024]{1,0:T(4,128)S(1)}, f32[4,1024]{1,0:T(4,128)}, u32[]{:S(2)}) copy-start(f32[4,1024]{1,0:T(4,128)} %bias.1) | copy-start | bytes 49156
  15.6 11.1 %copy-start.5 = (f32[1024]{0:T(1024)S(1)}, f32[1024]{0:T(1024)}, u32[]{:S(2)}) copy-start(f32[1024]{0:T(1024)} %param.17) | copy-start | bytes 12292
  26.7 21.8 %copy-start.2 = (bf16[32,256]{1,0:T(8,128)(2,1)S(1)}, bf16[32,256]{1,0:T(8,128)(2,1)}, u32[]{:S(2)}) copy-start(bf16[32,256]{1,0:T(8,128)(2,1)} %user.1) | copy-start | bytes 49156
  26.7 21.8 %copy-start.3 = (s32[4096,32]{0,1:T(8,128)S(1)}, s32[4096,32]{0,1:T(8,128)}, u32[]{:S(2)}) copy-start(s32[4096,32]{0,1:T(8,128)} %param.11) | copy-start | bytes 1572868
  44.3 13.9 %copy-start.1 = (s32[512,128]{1,0:T(8,128)S(1)}, s32[512,128]{1,0:T(8,128)}, u32[]{:S(2)}) copy-start(s32[512,128]{1,0:T(8,128)} %get-tuple-element.5.meta) | copy-start | bytes 786436
  44.3 13.9 %all-to-all-start.1 = ((f32[128,1,128]{2,1,0:T(1,128)}), f32[128,1,128]{2,1,0:T(1,128)S(1)}, u32[]{:S(2)}, u32[]{:S(2)}) async-start(f32[128,1,128]{2,1,0:T(1,128)} %rank.1), calls=%async_computation.1 | async-start | bytes 131072 | tf_op jit(solution)/shard_map/all_to_all | solution.py:500
